TPU v7x, 128 devices: a whole 4x4x4 slice. The times are simulated.
128 devices in a mesh: gy: 8 (over y_lo, z), gx: 16 (over y_hi, x, core).
Axes of the slice: x: 4, y: 4 (y_hi: 2, y_lo: 2; y = y_hi * 2 + y_lo), z: 4, core: 2. Of those that a mesh axis runs over, the one named last changes fastest.
Arguments:
- base_prod: bfloat16 [8, 1024, 4096], P(None, 'gy', 'gx'), may hold values from 0.5 to 2
- resident: float32 [1024, 4096], P('gy', 'gx'), may hold values from 0.2 to 5
- floor_space: float32 [1024, 4096], P('gy', 'gx'), may hold values from 0.5 to 2
- bracket: int32 [1024, 4096], P('gy', 'gx'), may hold values from 0 to 7
- tax_rate: float32 [8], replicated, may hold values from 0.05 to 0.45
- mixing: float32 [8, 8], replicated, may hold values from 0.02 to 0.2
- spill_decay: float32 [8], replicated, may hold values from 0.5 to 4
- commute_decay: float32 [8], replicated, may hold values from 0.5 to 4
- pair_dest: int32 [65536, 1], P(('gy', 'gx')), may hold values from 0 to 127; in each aligned block of 512 rows (0 to 511, 512 to 1023, ...) at most 8 rows name the same one
- pair_src: int32 [65536], P(('gy', 'gx')), may hold values from 0 to 2047
- pair_dst: int32 [65536], P(('gy', 'gx')), may hold values from 0 to 2047
- pair_count: int32 [65536], P(('gy', 'gx')), may hold values from 1 to 8
Outputs:
- wage_level: float32 [8, 1024, 4096], P(None, 'gy', 'gx')
- rent_level: float32 [1024, 4096], P('gy', 'gx')
Inputs may be any that keep to these rules, and one draw needn't show every extreme that they name: `pair_dest`: pair p leaves tile p // 512; among the pairs of one anchor tile no destination tile is named more than 8 times.
All inputs are finite; a program needn't handle non-finite values.
Results may differ from a plain program's by a relative error of at most 0.0003.
Values may be sent and summed in bfloat16 or wider, within the bound.
A program may use at most 64 MiB of HBM per device.

v0:
```python
import jax
import jax.numpy as jnp
from jax import lax
from jax.sharding import PartitionSpec as P

HALF = 64
ITERS = 3


BETA_WAGE = 0.3
FAR_SCALE = 0.125


def extended(block, sides, width):
    for axis, dim in sides:
        count = lax.axis_size(axis)
        forward = [(i, i + 1) for i in range(count - 1)]
        backward = [(target, source) for source, target in forward]
        low = lax.ppermute(
            lax.slice_in_dim(block, block.shape[dim] - width, None, axis=dim), axis, forward
        )
        high = lax.ppermute(lax.slice_in_dim(block, 0, width, axis=dim), axis, backward)
        block = jnp.concatenate([low, block, high], axis=dim)
    return block


def tap_bands(decay_rate):
    offset = jnp.abs(jnp.arange(2 * HALF + 1).astype(jnp.float32) - HALF) / HALF
    unscaled = jnp.exp(-decay_rate[:, None] * offset[None, :])
    tap_row = (unscaled / jnp.sum(unscaled, axis=1, keepdims=True)).astype(jnp.bfloat16)
    block_size = 2 * HALF
    tap_lag = jnp.arange(2 * block_size)[:, None] - jnp.arange(block_size)[None, :]
    inside = (tap_lag >= 0) & (tap_lag <= 2 * HALF)
    picked = tap_row[:, jnp.clip(tap_lag, 0, 2 * HALF)]
    banded = jnp.where(inside[None], picked, jnp.zeros_like(picked))
    return (banded[:, :block_size], banded[:, block_size:])


def column_pass(source, kernel_pair):
    block_size = 2 * HALF
    sectors, height = (source.shape[0], source.shape[1])
    blocks = source.reshape(sectors, height, -1, block_size)
    result = jnp.einsum(
        "synk,skc->sync", blocks[:, :, :-1], kernel_pair[0], preferred_element_type=jnp.float32
    )
    result = result + jnp.einsum(
        "synk,skc->sync", blocks[:, :, 1:], kernel_pair[1], preferred_element_type=jnp.float32
    )
    return result.reshape(sectors, height, -1)


def row_pass(source, kernel_pair):
    block_size = 2 * HALF
    sectors, breadth = (source.shape[0], source.shape[2])
    blocks = source.reshape(sectors, -1, block_size, breadth)
    result = jnp.einsum(
        "snkx,skc->sncx", blocks[:, :-1], kernel_pair[0], preferred_element_type=jnp.float32
    )
    result = result + jnp.einsum(
        "snkx,skc->sncx", blocks[:, 1:], kernel_pair[1], preferred_element_type=jnp.float32
    )
    return result.reshape(sectors, -1, breadth)


def correlate(source, kernel_pair):
    padded = extended(source, (("gy", 1), ("gx", 2)), HALF)
    tall_field = column_pass(padded, kernel_pair).astype(jnp.bfloat16)
    return row_pass(tall_field, kernel_pair)


def rent_step(rent_level, resident, floor_space, tax_cell, income, transfer):
    net_income = (1.0 - tax_cell) * income + transfer
    return jnp.sqrt(rent_level * resident * net_income / floor_space)


def body(
    base_prod,
    resident,
    floor_space,
    bracket,
    tax_rate,
    mixing,
    spill_decay,
    commute_decay,
    pair_dest,
    pair_src,
    pair_dst,
    pair_count,
):
    sectors, row_count, col_count = base_prod.shape
    tiles_y = lax.axis_size("gy")
    tiles_x = lax.axis_size("gx")
    devices = tiles_y * tiles_x
    pair_total = pair_src.shape[0]
    capacity = max(4, 2 * pair_total // devices)
    strips = row_count * (col_count // 16)
    lane_width = sectors * 16
    slot_total = devices * capacity
    kernel_comm = tap_bands(commute_decay)
    kernel_spill = tap_bands(spill_decay)
    destination = pair_dest[:, 0]
    device_ids = jnp.arange(devices, dtype=jnp.int32)
    onehot = (destination[:, None] == device_ids[None, :]).astype(jnp.int32)
    rank_in = jnp.sum(jnp.cumsum(onehot, axis=0) * onehot, axis=1) - 1
    slot_of = destination * capacity + rank_in
    routing = (
        jnp.zeros((slot_total, 2), jnp.int32)
        .at[slot_of]
        .set(jnp.stack([pair_dst, pair_count], axis=1))
    )
    routing = lax.all_to_all(
        routing.reshape(devices, capacity, 2), ("gy", "gx"), split_axis=0, concat_axis=0, tiled=True
    )
    routing = routing.reshape(slot_total, 2)
    target = routing[:, 0]
    weight = routing[:, 1].astype(jnp.float32)
    slot_ids = jnp.arange(slot_total, dtype=jnp.int32)
    strip_ids = jnp.arange(strips, dtype=jnp.int32)
    slot_hot = (slot_of[:, None] == slot_ids[None, :]).astype(jnp.bfloat16)
    source_hot = (pair_src[:, None] == strip_ids[None, :]).astype(jnp.bfloat16)
    send_matrix = lax.dot_general(
        slot_hot, source_hot, (((0,), (0,)), ((), ())), preferred_element_type=jnp.float32
    ).astype(jnp.bfloat16)
    receive_matrix = jnp.where(strip_ids[:, None] == target[None, :], weight[None, :], 0.0).astype(
        jnp.bfloat16
    )
    brackets = tax_rate.shape[0]
    bracket_ids = jnp.arange(brackets, dtype=jnp.int32)
    tax_cell = jnp.sum(
        jnp.where(bracket[None] == bracket_ids[:, None, None], tax_rate[:, None, None], 0.0), axis=0
    )
    base_float = base_prod.astype(jnp.float32)
    wage_level = base_float
    rent_level = jnp.ones_like(resident)
    population = None
    population = lax.psum(jnp.sum(resident), ("gy", "gx"))
    for iteration in range(ITERS):
        wage_power = wage_level * wage_level * wage_level
        sector_share = wage_power / jnp.sum(wage_power, axis=0)
        supply = (resident[None] * sector_share).astype(jnp.bfloat16)
        strip_table = (
            supply.reshape(sectors, row_count, col_count // 16, 16)
            .transpose(1, 2, 0, 3)
            .reshape(strips, lane_width)
        )
        outgoing = jnp.dot(send_matrix, strip_table, preferred_element_type=jnp.float32).astype(
            jnp.bfloat16
        )
        arrived = lax.all_to_all(
            outgoing.reshape(devices, capacity, lane_width),
            ("gy", "gx"),
            split_axis=0,
            concat_axis=0,
            tiled=True,
        )
        arrived = arrived.reshape(slot_total, lane_width)
        accumulated = jnp.dot(receive_matrix, arrived, preferred_element_type=jnp.float32)
        accumulated = accumulated.reshape(row_count, col_count // 16, sectors, 16).transpose(
            2, 0, 1, 3
        )
        far_flow = accumulated.reshape(sectors, row_count, col_count)
        near_flow = correlate(supply, kernel_comm)
        labor_force = near_flow + FAR_SCALE * far_flow
        spillover = correlate(labor_force.astype(jnp.bfloat16), kernel_spill)
        log_spill = jnp.log(1.0 + spillover).reshape(sectors, -1)
        mixed_logs = jnp.dot(mixing, log_spill, precision=lax.Precision.HIGHEST).reshape(
            sectors, row_count, col_count
        )
        productivity = base_float * jnp.exp(mixed_logs)
        income = jnp.sum(sector_share * wage_level, axis=0)
        revenue = lax.psum(jnp.sum(resident * tax_cell * income), ("gy", "gx"))
        rent_level = rent_step(
            rent_level, resident, floor_space, tax_cell, income, revenue / population
        )
        wage_level = productivity * jnp.exp(-BETA_WAGE * jnp.log(1.0 + labor_force))
    return (wage_level, rent_level)


def solution(mesh):
    return jax.shard_map(
        body,
        mesh=mesh,
        in_specs=(
            P(None, "gy", "gx"),
            P("gy", "gx"),
            P("gy", "gx"),
            P("gy", "gx"),
            P(),
            P(),
            P(),
            P(),
            P(("gy", "gx"), None),
            P(("gy", "gx")),
            P(("gy", "gx")),
            P(("gy", "gx")),
        ),
        out_specs=(P(None, "gy", "gx"), P("gy", "gx")),
        check_vma=False,
    )
```

profile of v0, /device:TPU:24, one launch (start us, length us, event | category | flops | bytes accessed | tf_op | source)
XLA Modules:
  0.0 665.2 jit_solution(1023174315598292874)
XLA Ops:
  16.6 8.1 %all-to-all-start = ((s32[128,8,2]{1,2,0:T(2,128)}), s32[128,8,2]{1,2,0:T(2,128)S(1)}, u32[]{:S(2)}, u32[]{:S(2)}) async-start(s32[128,8,2]{1,2,0:T(2,128)} %copy.339), calls=%async_computation | async-start | bytes 262144 | tf_op jit(solution)/shard_map/all_to_all | solution.py:111
  26.2 114.2 %gather_fusion = bf16[32768,8]{1,0:T(8,128)(2,1)} fusion(bf16[8,129]{0,1:T(8,128)(2,1)S(1)} %copy.323, s32[32768]{0:T(1024)S(1)} %fusion.93), kind=kCustom, calls=%fused_computation | custom fusion | bytes 1179648 | tf_op jit(solution)/shard_map/gather | solution.py:34
  140.4 6.8 %copy.413 = bf16[256,128,8]{1,0,2:T(8,128)(2,1)S(1)} copy(bf16[256,128,8]{2,1,0:T(8,128)(2,1)} %bitcast.271) | data formatting | bytes 1048576 | tf_op jit(solution)/shard_map/gather | solution.py:34
  147.3 114.2 %gather_fusion.1 = bf16[32768,8]{1,0:T(8,128)(2,1)} fusion(bf16[8,129]{0,1:T(8,128)(2,1)S(1)} %copy.325, s32[32768]{0:T(1024)S(1)} %fusion.93), kind=kCustom, calls=%fused_computation.1 | custom fusion | bytes 1179648 | tf_op jit(solution)/shard_map/gather | solution.py:34
  261.5 6.8 %copy.414 = bf16[256,128,8]{1,0,2:T(8,128)(2,1)S(1)} copy(bf16[256,128,8]{2,1,0:T(8,128)(2,1)} %bitcast.270) | data formatting | bytes 1048576 | tf_op jit(solution)/shard_map/gather | solution.py:34
  268.3 6.4 copy.342
  284.6 9.8 %all-to-all-start.1 = ((bf16[128,8,128]{2,1,0:T(8,128)(2,1)}), bf16[128,8,128]{2,1,0:T(8,128)(2,1)S(1)}, u32[]{:S(2)}, u32[]{:S(2)}) async-start(bf16[128,8,128]{2,1,0:T(8,128)(2,1)} %fusion.51), calls=%async_computation.1 | async-start | bytes 524288 | tf_op jit(solution)/shard_map/all_to_all | solution.py:149
  294.6 9.0 %all-to-all-done.1 = bf16[128,8,128]{2,1,0:T(8,128)(2,1)S(1)} async-done(((bf16[128,8,128]{2,1,0:T(8,128)(2,1)}), bf16[128,8,128]{2,1,0:T(8,128)(2,1)S(1)}, u32[]{:S(2)}, u32[]{:S(2)}) %all-to-all-start.1) | async-done | bytes 262176 | tf_op jit(solution)/shard_map/all_to_all | solution.py:149
  307.1 7.2 %collective-permute-start.3 = (bf16[8,256,64]{2,1,0:T(8,128)(2,1)}, bf16[8,256,64]{2,1,0:T(8,128)(2,1)}, u32[]{:S(2)}, u32[]{:S(2)}) collective-permute-start(bf16[8,256,64]{2,1,0:T(8,128)(2,1)} %get-tuple-element.33), channel_id=1, source_target_pairs={{1,0},{2,1},{3,2},{4,3},{5,4},{6,5},{7,6},{8,7},{9,8},{10,9},{11,1... | collective-permute-start | bytes 786440 | tf_op jit(solution)/shard_map/ppermute | solution.py:22
  335.8 5.2 collective-permute-start.5
  347.1 7.7 %collective-permute-start.7 = (bf16[8,256,64]{2,1,0:T(8,128)(2,1)S(1)}, bf16[8,256,64]{2,1,0:T(8,128)(2,1)S(1)}, u32[]{:S(2)}, u32[]{:S(2)}) collective-permute-start(bf16[8,256,64]{2,1,0:T(8,128)(2,1)S(1)} %get-tuple-element.31), channel_id=1, source_target_pairs={{1,0},{2,1},{3,2},{4,3},{5,4},{6,5},{7,6},{8,7},{9,8},{10,9},{11,1... | collective-permute-start | bytes 786440 | tf_op jit(solution)/shard_map/ppermute | solution.py:22
  375.2 6.3 collective-permute-start.9
  381.5 6.4 copy.363
  396.5 16.6 %all_to_all.20 = bf16[128,8,128]{2,1,0:T(8,128)(2,1)S(1)} all-to-all(bf16[128,8,128]{2,1,0:T(8,128)(2,1)S(1)} %fusion.52), channel_id=1, replica_groups=mesh['gy'=8,'gx'=16] {'gy','gx'}, dimensions={0} | all-to-all | bytes 524288 | tf_op jit(solution)/shard_map/all_to_all | solution.py:149
  416.6 7.3 %collective-permute-start.11 = (bf16[8,256,64]{2,1,0:T(8,128)(2,1)}, bf16[8,256,64]{2,1,0:T(8,128)(2,1)}, u32[]{:S(2)}, u32[]{:S(2)}) collective-permute-start(bf16[8,256,64]{2,1,0:T(8,128)(2,1)} %get-tuple-element.29), channel_id=1, source_target_pairs={{1,0},{2,1},{3,2},{4,3},{5,4},{6,5},{7,6},{8,7},{9,8},{10,9},{11,1... | collective-permute-start | bytes 786440 | tf_op jit(solution)/shard_map/ppermute | solution.py:22
  447.4 5.2 collective-permute-start.13
  458.7 7.3 %collective-permute-start.15 = (bf16[8,256,64]{2,1,0:T(8,128)(2,1)S(1)}, bf16[8,256,64]{2,1,0:T(8,128)(2,1)S(1)}, u32[]{:S(2)}, u32[]{:S(2)}) collective-permute-start(bf16[8,256,64]{2,1,0:T(8,128)(2,1)S(1)} %get-tuple-element.27), channel_id=1, source_target_pairs={{1,0},{2,1},{3,2},{4,3},{5,4},{6,5},{7,6},{8,7},{9,8},{10,9},{11,1... | collective-permute-start | bytes 786440 | tf_op jit(solution)/shard_map/ppermute | solution.py:22
  488.5 6.3 collective-permute-start.17
  494.8 6.4 copy.384
  509.8 16.6 %all_to_all.21 = bf16[128,8,128]{2,1,0:T(8,128)(2,1)S(1)} all-to-all(bf16[128,8,128]{2,1,0:T(8,128)(2,1)S(1)} %fusion.53), channel_id=1, replica_groups=mesh['gy'=8,'gx'=16] {'gy','gx'}, dimensions={0} | all-to-all | bytes 524288 | tf_op jit(solution)/shard_map/all_to_all | solution.py:149
  529.9 7.4 %collective-permute-start.19 = (bf16[8,256,64]{2,1,0:T(8,128)(2,1)}, bf16[8,256,64]{2,1,0:T(8,128)(2,1)}, u32[]{:S(2)}, u32[]{:S(2)}) collective-permute-start(bf16[8,256,64]{2,1,0:T(8,128)(2,1)} %get-tuple-element.25), channel_id=1, source_target_pairs={{1,0},{2,1},{3,2},{4,3},{5,4},{6,5},{7,6},{8,7},{9,8},{10,9},{11,1... | collective-permute-start | bytes 786440 | tf_op jit(solution)/shard_map/ppermute | solution.py:22
  560.7 5.3 collective-permute-start.21
  573.1 7.3 %collective-permute-start.23 = (bf16[8,256,64]{2,1,0:T(8,128)(2,1)}, bf16[8,256,64]{2,1,0:T(8,128)(2,1)}, u32[]{:S(2)}, u32[]{:S(2)}) collective-permute-start(bf16[8,256,64]{2,1,0:T(8,128)(2,1)} %get-tuple-element.23), channel_id=1, source_target_pairs={{1,0},{2,1},{3,2},{4,3},{5,4},{6,5},{7,6},{8,7},{9,8},{10,9},{11,1... | collective-permute-start | bytes 786440 | tf_op jit(solution)/shard_map/ppermute | solution.py:22
  581.2 65.3 %all-reduce = (f32[]{:T(128)}, f32[]{:T(128)}, f32[]{:T(128)}, f32[]{:T(128)}) all-reduce(f32[]{:T(128)} %get-tuple-element.4, f32[]{:T(128)} %get-tuple-element.5, f32[]{:T(128)} %get-tuple-element.3, f32[]{:T(128)} %get-tuple-element.2), channel_id=1, replica_groups=mesh['gy'=8,'gx'=16] {'gy','gx'}, use_global_device_ids=true, to_apply=%region_20.21 | all-reduce | flops 4 | bytes 32 | tf_op jit(solution)/shard_map/psum | solution.py:171
  (228 shorter events, 200.1 us)
Async XLA Ops:
  4.3 299.4 %collective-permute-start = (bf16[8,64,256]{2,1,0:T(8,128)(2,1)}, bf16[8,64,256]{2,1,0:T(8,128)(2,1)S(1)}, u32[]{:S(2)}, u32[]{:S(2)}) collective-permute-start(bf16[8,64,256]{2,1,0:T(8,128)(2,1)} %get-tuple-element.46), channel_id=1, source_target_pairs={{0,16},{16,32},{32,48},{48,64},{64,80},{80,96},{96,112},{1,17},{17... | collective-permute-start | bytes 786440 | tf_op jit(solution)/shard_map/ppermute | solution.py:19
  8.2 295.6 %collective-permute-start.1 = (bf16[8,64,256]{2,1,0:T(8,128)(2,1)}, bf16[8,64,256]{2,1,0:T(8,128)(2,1)S(1)}, u32[]{:S(2)}, u32[]{:S(2)}) collective-permute-start(bf16[8,64,256]{2,1,0:T(8,128)(2,1)} %get-tuple-element.47), channel_id=1, source_target_pairs={{16,0},{32,16},{48,32},{64,48},{80,64},{96,80},{112,96},{17,1},{33... | collective-permute-start | bytes 786440 | tf_op jit(solution)/shard_map/ppermute | solution.py:22
  16.6 268.0 %all-to-all-start = ((s32[128,8,2]{1,2,0:T(2,128)}), s32[128,8,2]{1,2,0:T(2,128)S(1)}, u32[]{:S(2)}, u32[]{:S(2)}) async-start(s32[128,8,2]{1,2,0:T(2,128)} %copy.339), calls=%async_computation | async-start | bytes 262144 | tf_op jit(solution)/shard_map/all_to_all | solution.py:111
  284.6 18.9 %all-to-all-start.1 = ((bf16[128,8,128]{2,1,0:T(8,128)(2,1)}), bf16[128,8,128]{2,1,0:T(8,128)(2,1)S(1)}, u32[]{:S(2)}, u32[]{:S(2)}) async-start(bf16[128,8,128]{2,1,0:T(8,128)(2,1)} %fusion.51), calls=%async_computation.1 | async-start | bytes 524288 | tf_op jit(solution)/shard_map/all_to_all | solution.py:149
  305.1 14.4 %collective-permute-start.2 = (bf16[8,256,64]{2,1,0:T(8,128)(2,1)}, bf16[8,256,64]{2,1,0:T(8,128)(2,1)}, u32[]{:S(2)}, u32[]{:S(2)}) collective-permute-start(bf16[8,256,64]{2,1,0:T(8,128)(2,1)} %get-tuple-element.32), channel_id=1, source_target_pairs={{0,1},{1,2},{2,3},{3,4},{4,5},{5,6},{6,7},{7,8},{8,9},{9,10},{10,1... | collective-permute-start | bytes 786440 | tf_op jit(solution)/shard_map/ppermute | solution.py:19
  307.1 14.2 %collective-permute-start.3 = (bf16[8,256,64]{2,1,0:T(8,128)(2,1)}, bf16[8,256,64]{2,1,0:T(8,128)(2,1)}, u32[]{:S(2)}, u32[]{:S(2)}) collective-permute-start(bf16[8,256,64]{2,1,0:T(8,128)(2,1)} %get-tuple-element.33), channel_id=1, source_target_pairs={{1,0},{2,1},{3,2},{4,3},{5,4},{6,5},{7,6},{8,7},{9,8},{10,9},{11,1... | collective-permute-start | bytes 786440 | tf_op jit(solution)/shard_map/ppermute | solution.py:22
  333.0 10.4 %collective-permute-start.4 = (bf16[8,64,256]{2,1,0:T(8,128)(2,1)S(1)}, bf16[8,64,256]{2,1,0:T(8,128)(2,1)S(1)}, u32[]{:S(2)}, u32[]{:S(2)}) collective-permute-start(bf16[8,64,256]{2,1,0:T(8,128)(2,1)S(1)} %get-tuple-element.44), channel_id=1, source_target_pairs={{0,16},{16,32},{32,48},{48,64},{64,80},{80,96},{96,112},{1,17},{17... | collective-permute-start | bytes 786440 | tf_op jit(solution)/shard_map/ppermute | solution.py:19
  345.2 14.1 %collective-permute-start.6 = (bf16[8,256,64]{2,1,0:T(8,128)(2,1)S(1)}, bf16[8,256,64]{2,1,0:T(8,128)(2,1)S(1)}, u32[]{:S(2)}, u32[]{:S(2)}) collective-permute-start(bf16[8,256,64]{2,1,0:T(8,128)(2,1)S(1)} %get-tuple-element.30), channel_id=1, source_target_pairs={{0,1},{1,2},{2,3},{3,4},{4,5},{5,6},{6,7},{7,8},{8,9},{9,10},{10,1... | collective-permute-start | bytes 786440 | tf_op jit(solution)/shard_map/ppermute | solution.py:19
  347.1 13.9 %collective-permute-start.7 = (bf16[8,256,64]{2,1,0:T(8,128)(2,1)S(1)}, bf16[8,256,64]{2,1,0:T(8,128)(2,1)S(1)}, u32[]{:S(2)}, u32[]{:S(2)}) collective-permute-start(bf16[8,256,64]{2,1,0:T(8,128)(2,1)S(1)} %get-tuple-element.31), channel_id=1, source_target_pairs={{1,0},{2,1},{3,2},{4,3},{5,4},{6,5},{7,6},{8,7},{9,8},{10,9},{11,1... | collective-permute-start | bytes 786440 | tf_op jit(solution)/shard_map/ppermute | solution.py:22
  373.1 40.1 %collective-permute-start.8 = (bf16[8,64,256]{2,1,0:T(8,128)(2,1)}, bf16[8,64,256]{2,1,0:T(8,128)(2,1)S(1)}, u32[]{:S(2)}, u32[]{:S(2)}) collective-permute-start(bf16[8,64,256]{2,1,0:T(8,128)(2,1)} %get-tuple-element.42), channel_id=1, source_target_pairs={{0,16},{16,32},{32,48},{48,64},{64,80},{80,96},{96,112},{1,17},{17... | collective-permute-start | bytes 786440 | tf_op jit(solution)/shard_map/ppermute | solution.py:19
  375.2 38.1 %collective-permute-start.9 = (bf16[8,64,256]{2,1,0:T(8,128)(2,1)}, bf16[8,64,256]{2,1,0:T(8,128)(2,1)S(1)}, u32[]{:S(2)}, u32[]{:S(2)}) collective-permute-start(bf16[8,64,256]{2,1,0:T(8,128)(2,1)} %get-tuple-element.43), channel_id=1, source_target_pairs={{16,0},{32,16},{48,32},{64,48},{80,64},{96,80},{112,96},{17,1},{33... | collective-permute-start | bytes 786440 | tf_op jit(solution)/shard_map/ppermute | solution.py:22
  414.6 14.4 %collective-permute-start.10 = (bf16[8,256,64]{2,1,0:T(8,128)(2,1)}, bf16[8,256,64]{2,1,0:T(8,128)(2,1)}, u32[]{:S(2)}, u32[]{:S(2)}) collective-permute-start(bf16[8,256,64]{2,1,0:T(8,128)(2,1)} %get-tuple-element.28), channel_id=1, source_target_pairs={{0,1},{1,2},{2,3},{3,4},{4,5},{5,6},{6,7},{7,8},{8,9},{9,10},{10,1... | collective-permute-start | bytes 786440 | tf_op jit(solution)/shard_map/ppermute | solution.py:19
  416.6 14.2 %collective-permute-start.11 = (bf16[8,256,64]{2,1,0:T(8,128)(2,1)}, bf16[8,256,64]{2,1,0:T(8,128)(2,1)}, u32[]{:S(2)}, u32[]{:S(2)}) collective-permute-start(bf16[8,256,64]{2,1,0:T(8,128)(2,1)} %get-tuple-element.29), channel_id=1, source_target_pairs={{1,0},{2,1},{3,2},{4,3},{5,4},{6,5},{7,6},{8,7},{9,8},{10,9},{11,1... | collective-permute-start | bytes 786440 | tf_op jit(solution)/shard_map/ppermute | solution.py:22
  444.6 10.4 %collective-permute-start.12 = (bf16[8,64,256]{2,1,0:T(8,128)(2,1)S(1)}, bf16[8,64,256]{2,1,0:T(8,128)(2,1)S(1)}, u32[]{:S(2)}, u32[]{:S(2)}) collective-permute-start(bf16[8,64,256]{2,1,0:T(8,128)(2,1)S(1)} %get-tuple-element.40), channel_id=1, source_target_pairs={{0,16},{16,32},{32,48},{48,64},{64,80},{80,96},{96,112},{1,17},{17... | collective-permute-start | bytes 786440 | tf_op jit(solution)/shard_map/ppermute | solution.py:19
  456.8 14.1 %collective-permute-start.14 = (bf16[8,256,64]{2,1,0:T(8,128)(2,1)S(1)}, bf16[8,256,64]{2,1,0:T(8,128)(2,1)S(1)}, u32[]{:S(2)}, u32[]{:S(2)}) collective-permute-start(bf16[8,256,64]{2,1,0:T(8,128)(2,1)S(1)} %get-tuple-element.26), channel_id=1, source_target_pairs={{0,1},{1,2},{2,3},{3,4},{4,5},{5,6},{6,7},{7,8},{8,9},{9,10},{10,1... | collective-permute-start | bytes 786440 | tf_op jit(solution)/shard_map/ppermute | solution.py:19
  458.7 13.9 %collective-permute-start.15 = (bf16[8,256,64]{2,1,0:T(8,128)(2,1)S(1)}, bf16[8,256,64]{2,1,0:T(8,128)(2,1)S(1)}, u32[]{:S(2)}, u32[]{:S(2)}) collective-permute-start(bf16[8,256,64]{2,1,0:T(8,128)(2,1)S(1)} %get-tuple-element.27), channel_id=1, source_target_pairs={{1,0},{2,1},{3,2},{4,3},{5,4},{6,5},{7,6},{8,7},{9,8},{10,9},{11,1... | collective-permute-start | bytes 786440 | tf_op jit(solution)/shard_map/ppermute | solution.py:22
  486.4 40.1 %collective-permute-start.16 = (bf16[8,64,256]{2,1,0:T(8,128)(2,1)}, bf16[8,64,256]{2,1,0:T(8,128)(2,1)S(1)}, u32[]{:S(2)}, u32[]{:S(2)}) collective-permute-start(bf16[8,64,256]{2,1,0:T(8,128)(2,1)} %get-tuple-element.38), channel_id=1, source_target_pairs={{0,16},{16,32},{32,48},{48,64},{64,80},{80,96},{96,112},{1,17},{17... | collective-permute-start | bytes 786440 | tf_op jit(solution)/shard_map/ppermute | solution.py:19
  488.5 38.1 %collective-permute-start.17 = (bf16[8,64,256]{2,1,0:T(8,128)(2,1)}, bf16[8,64,256]{2,1,0:T(8,128)(2,1)S(1)}, u32[]{:S(2)}, u32[]{:S(2)}) collective-permute-start(bf16[8,64,256]{2,1,0:T(8,128)(2,1)} %get-tuple-element.39), channel_id=1, source_target_pairs={{16,0},{32,16},{48,32},{64,48},{80,64},{96,80},{112,96},{17,1},{33... | collective-permute-start | bytes 786440 | tf_op jit(solution)/shard_map/ppermute | solution.py:22
  527.9 14.4 %collective-permute-start.18 = (bf16[8,256,64]{2,1,0:T(8,128)(2,1)}, bf16[8,256,64]{2,1,0:T(8,128)(2,1)}, u32[]{:S(2)}, u32[]{:S(2)}) collective-permute-start(bf16[8,256,64]{2,1,0:T(8,128)(2,1)} %get-tuple-element.24), channel_id=1, source_target_pairs={{0,1},{1,2},{2,3},{3,4},{4,5},{5,6},{6,7},{7,8},{8,9},{9,10},{10,1... | collective-permute-start | bytes 786440 | tf_op jit(solution)/shard_map/ppermute | solution.py:19
  529.9 14.2 %collective-permute-start.19 = (bf16[8,256,64]{2,1,0:T(8,128)(2,1)}, bf16[8,256,64]{2,1,0:T(8,128)(2,1)}, u32[]{:S(2)}, u32[]{:S(2)}) collective-permute-start(bf16[8,256,64]{2,1,0:T(8,128)(2,1)} %get-tuple-element.25), channel_id=1, source_target_pairs={{1,0},{2,1},{3,2},{4,3},{5,4},{6,5},{7,6},{8,7},{9,8},{10,9},{11,1... | collective-permute-start | bytes 786440 | tf_op jit(solution)/shard_map/ppermute | solution.py:22
  557.9 10.4 %collective-permute-start.20 = (bf16[8,64,256]{2,1,0:T(8,128)(2,1)S(1)}, bf16[8,64,256]{2,1,0:T(8,128)(2,1)S(1)}, u32[]{:S(2)}, u32[]{:S(2)}) collective-permute-start(bf16[8,64,256]{2,1,0:T(8,128)(2,1)S(1)} %get-tuple-element.36), channel_id=1, source_target_pairs={{0,16},{16,32},{32,48},{48,64},{64,80},{80,96},{96,112},{1,17},{17... | collective-permute-start | bytes 786440 | tf_op jit(solution)/shard_map/ppermute | solution.py:19
  560.7 9.2 %collective-permute-start.21 = (bf16[8,64,256]{2,1,0:T(8,128)(2,1)S(1)}, bf16[8,64,256]{2,1,0:T(8,128)(2,1)S(1)}, u32[]{:S(2)}, u32[]{:S(2)}) collective-permute-start(bf16[8,64,256]{2,1,0:T(8,128)(2,1)S(1)} %get-tuple-element.37), channel_id=1, source_target_pairs={{16,0},{32,16},{48,32},{64,48},{80,64},{96,80},{112,96},{17,1},{33... | collective-permute-start | bytes 786440 | tf_op jit(solution)/shard_map/ppermute | solution.py:22
  571.2 79.8 %collective-permute-start.22 = (bf16[8,256,64]{2,1,0:T(8,128)(2,1)}, bf16[8,256,64]{2,1,0:T(8,128)(2,1)S(1)}, u32[]{:S(2)}, u32[]{:S(2)}) collective-permute-start(bf16[8,256,64]{2,1,0:T(8,128)(2,1)} %get-tuple-element.22), channel_id=1, source_target_pairs={{0,1},{1,2},{2,3},{3,4},{4,5},{5,6},{6,7},{7,8},{8,9},{9,10},{10,1... | collective-permute-start | bytes 786440 | tf_op jit(solution)/shard_map/ppermute | solution.py:19
  573.1 77.9 %collective-permute-start.23 = (bf16[8,256,64]{2,1,0:T(8,128)(2,1)}, bf16[8,256,64]{2,1,0:T(8,128)(2,1)}, u32[]{:S(2)}, u32[]{:S(2)}) collective-permute-start(bf16[8,256,64]{2,1,0:T(8,128)(2,1)} %get-tuple-element.23), channel_id=1, source_target_pairs={{1,0},{2,1},{3,2},{4,3},{5,4},{6,5},{7,6},{8,7},{9,8},{10,9},{11,1... | collective-permute-start | bytes 786440 | tf_op jit(solution)/shard_map/ppermute | solution.py:22
  (31 other events, 652.8 us)
where the time goes:
time: 677 us; the launch traced here: 665 us
  local copies, waits for them, and re-layouts  329 us (49%)
  starting transfers between devices  123 us (18%)
  blocking collectives  98.5 us (15%)
  waiting for transfers between devices  45.1 us (7%)
  matrix products  35 us (5%)
  other arithmetic  28.7 us (4%)
    gather x4, local copies, waits for them, and re-layouts, tap_bands(): picked = tap_row[:, jnp.clip(tap_lag, 0, 2 * HALF)]  242 us
    ppermute x12, starting transfers between devices, extended(): lax.ppermute(lax.slice_in_dim(block, 0, width, axis=dim), axis, backward)  76.7 us
    psum x1, blocking collectives, body(): revenue = lax.psum(jnp.sum(resident * tax_cell * income), ('gy', 'gx'))  65.3 us
    all_to_all x2, blocking collectives, body(): lax.all_to_all(outgoing.reshape(devices, capacity, lane_width), ('gy', 'g...  33.1 us
    ppermute x12, starting transfers between devices, extended(): lax.ppermute(lax.slice_in_dim(block, block.shape[dim] - width, None, axis...  28 us
    ppermute x12, waiting for transfers between devices, extended(): lax.ppermute(lax.slice_in_dim(block, block.shape[dim] - width, None, axis...  22.8 us
    convert_element_type x12, local copies, waits for them, and re-layouts, correlate(): tall_field = column_pass(padded, kernel_pair).astype(jnp.bfloat16)  22.7 us
    transpose x3, local copies, waits for them, and re-layouts, body(): strip_table = supply.reshape(sectors, row_count, col_count // 16, 16).tra...  19.3 us
  transfers between devices with their start and end apart: 26, of which 17 were waited for; matrix products, arithmetic and copies ran while one was open for 46% of the time, Pallas kernels for 0%

commit v1 on v0

v1 whole, which is shorter than its diff:
```python
import functools

import jax
import jax.numpy as jnp
from jax import lax
from jax.experimental import pallas as pl
from jax.experimental.pallas import tpu as pltpu
from jax.sharding import PartitionSpec as P

HALF = 64
ITERS = 3
SECTORS = 8
CAP = 8
BETA_WAGE = 0.3
FAR_SCALE = 0.125
ROWS = 128
COLS = 256
GROUPS = COLS // 16
PAIRS2 = SECTORS // 2
CHUNK = 16
MESH = pl.DeviceIdType.MESH
F32 = jnp.float32
BF16 = jnp.bfloat16


def swap_blocks(values):
    values = list(values)
    block = lax.broadcasted_iota(jnp.int32, values[0].shape, 1) // 16
    for d in (1, 2, 4):
        low = (block & d) == 0
        for a in range(8):
            if a & d:
                continue
            b = a + d
            first, second = values[a], values[b]
            values[a] = jnp.where(low, first, pltpu.roll(second, 16 * d, 1))
            values[b] = jnp.where(low, pltpu.roll(first, 128 - 16 * d, 1), second)
    return values


def kernel(
    tiles_y,
    tiles_x,
    base_ref,
    resident_ref,
    floor_ref,
    bracket_ref,
    pairs_ref,
    tax_ref,
    mixing_ref,
    spill_ref,
    commute_ref,
    wage_ref,
    rent_ref,
    ext,
    edge_out,
    edge_in,
    mid,
    near,
    labor,
    tap_row,
    band_row,
    band_col,
    band_edge,
    table,
    source_hot,
    slot_hot,
    place,
    far,
    one_out,
    one_in,
    two_out,
    two_in,
    sum_out,
    sum_in,
    total_out,
    total_in,
    rate_ref,
    income_ref,
    row_send,
    row_recv,
    edge_send,
    edge_recv,
    one_send,
    one_recv,
    two_send,
    two_recv,
    sum_send,
    sum_recv,
):
    my = lax.axis_index("gy")
    mx = lax.axis_index("gx")
    slots_x = tiles_y * CAP
    slots_y = tiles_x * CAP
    slots = tiles_x * slots_x
    far_pairs = pairs_ref.shape[1]

    barrier = pltpu.get_barrier_semaphore()

    def greet_x(j, carry):
        pl.semaphore_signal(
            barrier, inc=1, device_id=(my, lax.rem(mx + j, tiles_x)), device_id_type=MESH
        )
        return carry

    def greet_y(j, carry):
        pl.semaphore_signal(
            barrier, inc=1, device_id=(lax.rem(my + j, tiles_y), mx), device_id_type=MESH
        )
        return carry

    lax.fori_loop(1, tiles_x, greet_x, 0)
    lax.fori_loop(1, tiles_y, greet_y, 0)

    @pl.when(my == 0)
    def _():
        ext[:, :, 0:HALF, :] = jnp.zeros((2 * ITERS, SECTORS, HALF, COLS), BF16)

    @pl.when(my == tiles_y - 1)
    def _():
        ext[:, :, HALF + ROWS :, :] = jnp.zeros((2 * ITERS, SECTORS, HALF, COLS), BF16)

    @pl.when(mx == 0)
    def _():
        edge_in[:, 0] = jnp.zeros((2 * ITERS, PAIRS2, ROWS, 128), BF16)

    @pl.when(mx == tiles_x - 1)
    def _():
        edge_in[:, 1] = jnp.zeros((2 * ITERS, PAIRS2, ROWS, 128), BF16)

    def row_copy(e, i, way):
        start = HALF if way == 0 else ROWS
        land = HALF + ROWS if way == 0 else 0
        target = my - 1 if way == 0 else my + 1
        return pltpu.make_async_remote_copy(
            src_ref=ext.at[e, pl.ds(2 * i, 2), pl.ds(start, HALF), :],
            dst_ref=ext.at[e, pl.ds(2 * i, 2), pl.ds(land, HALF), :],
            send_sem=row_send.at[e, way],
            recv_sem=row_recv.at[e, way, i],
            device_id=(target, mx),
            device_id_type=MESH,
        )

    def row_drain(e, way):
        start = HALF if way == 0 else ROWS
        target = my - 1 if way == 0 else my + 1
        return pltpu.make_async_remote_copy(
            src_ref=ext.at[e, :, pl.ds(start, HALF), :],
            dst_ref=ext.at[e, :, pl.ds(start, HALF), :],
            send_sem=row_send.at[e, way],
            recv_sem=row_recv.at[e, way, 0],
            device_id=(target, mx),
            device_id_type=MESH,
        )

    can_row = (my > 0, my < tiles_y - 1)
    can_edge = (mx > 0, mx < tiles_x - 1)

    def send_rows(e, way):
        @pl.when(can_row[way])
        def _():
            for i in range(PAIRS2):
                row_copy(e, i, way).start()

    def edge_copy(e, i, way):
        target = mx - 1 if way == 0 else mx + 1
        return pltpu.make_async_remote_copy(
            src_ref=edge_out.at[e, way, i],
            dst_ref=edge_in.at[e, 1 - way, i],
            send_sem=edge_send.at[e, way],
            recv_sem=edge_recv.at[e, way, i],
            device_id=(my, target),
            device_id_type=MESH,
        )

    def edge_drain(e, way):
        target = mx - 1 if way == 0 else mx + 1
        return pltpu.make_async_remote_copy(
            src_ref=edge_out.at[e, way],
            dst_ref=edge_in.at[e, 1 - way],
            send_sem=edge_send.at[e, way],
            recv_sem=edge_recv.at[e, way, 0],
            device_id=(my, target),
            device_id_type=MESH,
        )

    lane128 = lax.broadcasted_iota(jnp.int32, (ROWS, 128), 1)

    def rows_pass(e, kind):
        def one(i, carry):
            for way in range(2):

                @pl.when(can_row[1 - way])
                def _():
                    row_copy(e, i, way).wait_recv()

            ends = []
            for k in range(2):
                s = 2 * i + k
                passed = jnp.dot(
                    band_row[kind * SECTORS + s], ext[e, s], preferred_element_type=F32
                )
                mid[s] = passed.astype(BF16)
                ends.append((passed[:, 0:128], passed[:, 128:256]))
            first, second = ends
            low = lane128 < HALF
            edge_out[e, 0, i] = jnp.where(low, first[0], pltpu.roll(second[0], HALF, 1)).astype(
                BF16
            )
            edge_out[e, 1, i] = jnp.where(low, pltpu.roll(second[1], HALF, 1), first[1]).astype(
                BF16
            )
            for way in range(2):

                @pl.when(can_edge[way])
                def _():
                    edge_copy(e, i, way).start()

            return carry

        lax.fori_loop(0, PAIRS2, one, 0)

    def columns_pass(e, kind, result):
        def one(i, carry):
            for way in range(2):

                @pl.when(can_edge[1 - way])
                def _():
                    edge_copy(e, i, way).wait_recv()

            for k in range(2):
                s = 2 * i + k
                b = kind * SECTORS + s
                value = jnp.dot(mid[s], band_col[b], preferred_element_type=F32)
                value += jnp.dot(
                    edge_in[e, 0, i], band_edge[b, 0:128, :], preferred_element_type=F32
                )
                value += jnp.dot(
                    edge_in[e, 1, i], band_edge[b, 128:256, :], preferred_element_type=F32
                )
                result[s] = value
            return carry

        lax.fori_loop(0, PAIRS2, one, 0)

    def make_bands(kind):
        u = lax.broadcasted_iota(jnp.int32, (COLS, COLS), 0)
        x = lax.broadcasted_iota(jnp.int32, (COLS, COLS), 1)
        inside = jnp.abs(u - x) <= 128

        def one(s, carry):
            b = kind * SECTORS + s
            line = jnp.broadcast_to(tap_row[pl.ds(b, 1), :], (ROWS, COLS))
            rows_band = pltpu.roll(line, 0, 1, stride=1, stride_axis=0)
            band_row[b] = rows_band.astype(BF16)
            circle = jnp.concatenate(
                [pltpu.roll(rows_band, COLS - HALF, 1), pltpu.roll(rows_band, HALF, 1)], axis=0
            )
            band_col[b] = jnp.where(inside, circle, 0.0).astype(BF16)
            rest = jnp.where(inside, 0.0, circle)
            even = jnp.concatenate([rest[128:256], rest[0:128]], axis=0)
            odd = jnp.concatenate(
                [rest[192:256], rest[128:192], rest[64:128], rest[0:64]], axis=0
            )
            band_edge[b] = jnp.where(lax.rem(s, 2) == 0, even, odd).astype(BF16)
            return carry

        lax.fori_loop(0, SECTORS, one, 0)

    def first_copy(a, x):
        return pltpu.make_async_remote_copy(
            src_ref=one_out.at[a, x],
            dst_ref=one_in.at[a, mx],
            send_sem=one_send.at[a],
            recv_sem=one_recv.at[a],
            device_id=(my, x),
            device_id_type=MESH,
        )

    def first_all(a):
        return pltpu.make_async_remote_copy(
            src_ref=one_out.at[a, pl.ds(0, tiles_x - 1)],
            dst_ref=one_in.at[a, pl.ds(0, tiles_x - 1)],
            send_sem=one_send.at[a],
            recv_sem=one_recv.at[a],
            device_id=(my, lax.rem(mx + 1, tiles_x)),
            device_id_type=MESH,
        )

    def second_copy(a, y):
        return pltpu.make_async_remote_copy(
            src_ref=two_out.at[a, y],
            dst_ref=two_in.at[a, my],
            send_sem=two_send.at[a],
            recv_sem=two_recv.at[a],
            device_id=(y, mx),
            device_id_type=MESH,
        )

    def second_all(a):
        return pltpu.make_async_remote_copy(
            src_ref=two_out.at[a, pl.ds(0, tiles_y - 1)],
            dst_ref=two_in.at[a, pl.ds(0, tiles_y - 1)],
            send_sem=two_send.at[a],
            recv_sem=two_recv.at[a],
            device_id=(lax.rem(my + 1, tiles_y), mx),
            device_id_type=MESH,
        )

    def start_first(a):
        def one(j, carry):
            first_copy(a, lax.rem(mx + j, tiles_x)).start()
            return carry

        lax.fori_loop(1, tiles_x, one, 0)
        one_in[a, mx] = one_out[a, mx]

    def pass_on(a):
        first_all(a).wait_recv()
        for i in range(tiles_x // 2):
            pieces = [
                one_in[a, 2 * i + k].astype(F32).reshape(tiles_y, CAP, 128) for k in range(2)
            ]
            two_out[a, :, 2 * i * CAP : 2 * (i + 1) * CAP, :] = jnp.concatenate(
                pieces, axis=1
            ).astype(BF16)

        def one(j, carry):
            second_copy(a, lax.rem(my + j, tiles_y)).start()
            return carry

        lax.fori_loop(1, tiles_y, one, 0)
        two_in[a, my] = two_out[a, my]

    def sum_copy(x):
        return pltpu.make_async_remote_copy(
            src_ref=sum_out,
            dst_ref=sum_in.at[mx],
            send_sem=sum_send.at[0],
            recv_sem=sum_recv.at[0],
            device_id=(my, x),
            device_id_type=MESH,
        )

    def total_copy(y):
        return pltpu.make_async_remote_copy(
            src_ref=total_out,
            dst_ref=total_in.at[my],
            send_sem=sum_send.at[1],
            recv_sem=sum_recv.at[1],
            device_id=(y, mx),
            device_id_type=MESH,
        )

    def sum_all():
        return pltpu.make_async_remote_copy(
            src_ref=sum_in.at[pl.ds(0, tiles_x - 1)],
            dst_ref=sum_in.at[pl.ds(0, tiles_x - 1)],
            send_sem=sum_send.at[0],
            recv_sem=sum_recv.at[0],
            device_id=(my, lax.rem(mx + 1, tiles_x)),
            device_id_type=MESH,
        )

    def total_all():
        return pltpu.make_async_remote_copy(
            src_ref=total_in.at[pl.ds(0, tiles_y - 1)],
            dst_ref=total_in.at[pl.ds(0, tiles_y - 1)],
            send_sem=sum_send.at[1],
            recv_sem=sum_recv.at[1],
            device_id=(lax.rem(my + 1, tiles_y), mx),
            device_id_type=MESH,
        )

    def shares(it, r, h, wages, revenue):
        rows = pl.ds(r, CHUNK)
        lanes = slice(128 * h, 128 * h + 128)
        powers = [w * w * w for w in wages]
        inverse = 1.0 / sum(powers[1:], powers[0])
        people = resident_ref[rows, lanes]
        share = [p * inverse for p in powers]
        income = sum([q * w for q, w in zip(share[1:], wages[1:])], share[0] * wages[0])
        income_ref[it, rows, lanes] = income
        supply = [people * q for q in share]
        for s in range(SECTORS):
            ext[2 * it, s, pl.ds(HALF + r, CHUNK), lanes] = supply[s].astype(BF16)
        for g, strip in enumerate(swap_blocks(supply)):
            table[pl.ds((8 * h + g) * ROWS + r, CHUNK), :] = strip.astype(BF16)
        gain = people * rate_ref[rows, lanes] * income
        return revenue + gain[0:8] + gain[8:16]

    def gather(a):
        picked = jnp.dot(source_hot[...], table[...], preferred_element_type=F32).astype(BF16)
        ordered = jnp.dot(slot_hot[...], picked, preferred_element_type=F32).astype(BF16)
        one_out[a] = ordered.reshape(tiles_x, slots_x, 128)

    zero = jnp.zeros((8, 128), F32)

    def first_chunk(c, carry):
        people_sum, revenue = carry
        r = pl.multiple_of(c * CHUNK, CHUNK)
        rows = pl.ds(r, CHUNK)
        for h in range(2):
            lanes = slice(128 * h, 128 * h + 128)
            bracket = bracket_ref[rows, lanes]
            rate = jnp.zeros((CHUNK, 128), F32)
            for b in range(8):
                rate = jnp.where(bracket == b, tax_ref[b], rate)
            rate_ref[rows, lanes] = rate
            people = resident_ref[rows, lanes]
            people_sum = people_sum + people[0:8] + people[8:16]
            wages = [base_ref[s, rows, lanes].astype(F32) for s in range(SECTORS)]
            revenue = shares(0, r, h, wages, revenue)
        return people_sum, revenue

    people_sum, revenue0 = lax.fori_loop(0, ROWS // CHUNK, first_chunk, (zero, zero))
    pl.semaphore_wait(barrier, tiles_x - 1 + tiles_y - 1)
    send_rows(0, 0)
    send_rows(0, 1)

    across = pairs_ref[...].T
    dest_row, slot_base = pairs_ref[0:1, :], pairs_ref[1:2, :]
    earlier = lax.broadcasted_iota(jnp.int32, (far_pairs, far_pairs), 0) < (
        lax.broadcasted_iota(jnp.int32, (far_pairs, far_pairs), 1)
    )
    same = (across[:, 0:1] == dest_row) & earlier
    rank = jnp.sum(jnp.where(same, 1.0, 0.0), axis=0, keepdims=True)
    slot_of = (slot_base + rank).astype(jnp.int32)
    slot_ids = lax.broadcasted_iota(jnp.int32, (slots, far_pairs), 0)
    slot_hot[...] = jnp.where(slot_ids == slot_of, 1.0, 0.0).astype(BF16)
    strip_ids = lax.broadcasted_iota(jnp.int32, (far_pairs, GROUPS * ROWS), 1)
    source_hot[...] = jnp.where(
        strip_ids == across[:, 2:3].astype(jnp.int32), 1.0, 0.0
    ).astype(BF16)
    one_out[ITERS] = (
        jnp.dot(slot_hot[...], across.astype(BF16), preferred_element_type=F32)
        .astype(BF16)
        .reshape(tiles_x, slots_x, 128)
    )
    start_first(ITERS)
    gather(0)
    start_first(0)

    sector = lax.broadcasted_iota(jnp.int32, (2 * SECTORS, COLS), 0)
    tap = lax.broadcasted_iota(jnp.int32, (2 * SECTORS, COLS), 1)
    decay = jnp.zeros((2 * SECTORS, COLS), F32)
    for s in range(SECTORS):
        decay = jnp.where(sector == s, commute_ref[s], decay)
        decay = jnp.where(sector == SECTORS + s, spill_ref[s], decay)
    offset = jnp.abs(tap - HALF).astype(F32) / HALF
    unscaled = jnp.where(tap <= 2 * HALF, jnp.exp(-decay * offset), 0.0)
    tap_row[...] = (unscaled / jnp.sum(unscaled, axis=1, keepdims=True)).astype(BF16).astype(F32)
    make_bands(0)

    pass_on(ITERS)

    def build_place():
        second_all(ITERS).wait_recv()
        routing = two_in[ITERS].reshape(slots, 128)
        line = lax.broadcasted_iota(jnp.int32, (16, 128), 0)
        lane = lax.broadcasted_iota(jnp.int32, (16, 128), 1)
        pick = jnp.where((line == 0) & (lane == 3), 1.0, 0.0)
        pick = jnp.where((line == 0) & (lane == 4), float(ROWS), pick)
        pick = jnp.where((line == 1) & (lane == 5), 1.0, pick).astype(BF16)
        found = lax.dot_general(
            pick, routing, (((1,), (1,)), ((), ())), preferred_element_type=F32
        )
        where_to, weight = found[0:1, :].astype(jnp.int32), found[1:2, :]

        def one(g, carry):
            strip = g * ROWS + lax.broadcasted_iota(jnp.int32, (ROWS, slots), 0)
            place[pl.ds(pl.multiple_of(g * ROWS, ROWS), ROWS), :] = jnp.where(
                strip == where_to, weight, 0.0
            ).astype(BF16)
            return carry

        lax.fori_loop(0, GROUPS, one, 0)

    revenues = [revenue0]
    for it in range(ITERS):
        if it > 0:
            send_rows(2 * it, 0)
            send_rows(2 * it, 1)
            gather(it)
            start_first(it)
        if it == ITERS - 1:
            line = lax.broadcasted_iota(jnp.int32, (8, 128), 0)
            parts = zero
            for k, part in enumerate([people_sum] + revenues):
                parts = jnp.where(line == k, jnp.sum(part, axis=0, keepdims=True), parts)
            sum_out[...] = parts

            def start_sum(j, carry):
                sum_copy(lax.rem(mx + j, tiles_x)).start()
                return carry

            lax.fori_loop(1, tiles_x, start_sum, 0)
            sum_in[mx] = parts
        rows_pass(2 * it, 0)
        pass_on(it)
        if it == ITERS - 1:
            sum_all().wait_recv()
            halfway = jnp.sum(sum_in[...], axis=0)
            total_out[...] = halfway

            def start_total(j, carry):
                total_copy(lax.rem(my + j, tiles_y)).start()
                return carry

            lax.fori_loop(1, tiles_y, start_total, 0)
            total_in[my] = halfway
        columns_pass(2 * it, 0, near)
        if it == 0:
            build_place()
        second_all(it).wait_recv()
        far[...] = jnp.dot(
            place[...], two_in[it].reshape(slots, 128), preferred_element_type=F32
        )

        def labor_chunk(c, carry):
            r = pl.multiple_of(c * CHUNK, CHUNK)
            for h in range(2):
                lanes = slice(128 * h, 128 * h + 128)
                strips = [far[pl.ds((8 * h + g) * ROWS + r, CHUNK), :] for g in range(8)]
                for s, flow in enumerate(swap_blocks(strips)):
                    value = near[s, pl.ds(r, CHUNK), lanes] + FAR_SCALE * flow
                    labor[s, pl.ds(r, CHUNK), lanes] = value
                    ext[2 * it + 1, s, pl.ds(HALF + r, CHUNK), lanes] = value.astype(BF16)
            return carry

        lax.fori_loop(0, HALF // CHUNK, labor_chunk, 0)
        send_rows(2 * it + 1, 0)
        lax.fori_loop(HALF // CHUNK, ROWS // CHUNK, labor_chunk, 0)
        send_rows(2 * it + 1, 1)
        if it == 0:
            make_bands(1)
        if it == ITERS - 1:
            total_all().wait_recv()
            sums = jnp.sum(jnp.sum(total_in[...], axis=0), axis=1, keepdims=True)
            people_all = sums[0:1, 0:1]
            transfers = [sums[1 + k : 2 + k, 0:1] / people_all for k in range(ITERS)]

            def rent_chunk(c, carry):
                rows = pl.ds(pl.multiple_of(c * CHUNK, CHUNK), CHUNK)
                keep = 1.0 - rate_ref[rows, :]
                people, space = resident_ref[rows, :], floor_ref[rows, :]
                rent = None
                for k in range(ITERS):
                    net = keep * income_ref[k, rows, :] + transfers[k]
                    level = people if rent is None else rent * people
                    rent = jnp.sqrt(level * net / space)
                rent_ref[rows, :] = rent
                return carry

            lax.fori_loop(0, ROWS // CHUNK, rent_chunk, 0)
        rows_pass(2 * it + 1, 1)
        columns_pass(2 * it + 1, 1, near)

        def wage_chunk(c, revenue):
            r = pl.multiple_of(c * CHUNK, CHUNK)
            rows = pl.ds(r, CHUNK)
            for h in range(2):
                lanes = slice(128 * h, 128 * h + 128)
                logs = [jnp.log(1.0 + near[s, rows, lanes]) for s in range(SECTORS)]
                wages = []
                for s in range(SECTORS):
                    power = -BETA_WAGE * jnp.log(1.0 + labor[s, rows, lanes])
                    for t in range(SECTORS):
                        power = power + mixing_ref[s, t] * logs[t]
                    wages.append(base_ref[s, rows, lanes].astype(F32) * jnp.exp(power))
                if it == ITERS - 1:
                    for s in range(SECTORS):
                        wage_ref[s, rows, lanes] = wages[s]
                else:
                    revenue = shares(it + 1, r, h, wages, revenue)
            return revenue

        revenues.append(lax.fori_loop(0, ROWS // CHUNK, wage_chunk, zero))

    for e in range(2 * ITERS):
        for way in range(2):

            @pl.when(can_row[way])
            def _():
                row_drain(e, way).wait_send()

            @pl.when(can_edge[way])
            def _():
                edge_drain(e, way).wait_send()

    for a in range(ITERS + 1):
        first_all(a).wait_send()
        second_all(a).wait_send()
    sum_all().wait_send()
    total_all().wait_send()


def body(
    base_prod,
    resident,
    floor_space,
    bracket,
    tax_rate,
    mixing,
    spill_decay,
    commute_decay,
    pair_dest,
    pair_src,
    pair_dst,
    pair_count,
):
    tiles_y = lax.axis_size("gy")
    tiles_x = lax.axis_size("gx")
    slots = tiles_y * tiles_x * CAP
    far_pairs = pair_src.shape[0]
    dest = pair_dest[:, 0]
    pairs = jnp.stack(
        [
            dest,
            (dest % tiles_x) * (tiles_y * CAP) + (dest // tiles_x) * CAP,
            (pair_src % GROUPS) * ROWS + pair_src // GROUPS,
            pair_dst // GROUPS,
            pair_dst % GROUPS,
            pair_count,
        ],
        axis=0,
    ).astype(F32)
    pairs = jnp.pad(pairs, ((0, 122), (0, 0)))
    vmem = pl.BlockSpec(memory_space=pltpu.VMEM)
    smem = pl.BlockSpec(memory_space=pltpu.SMEM)
    exchanges = 2 * ITERS
    dma = pltpu.SemaphoreType.DMA
    return pl.pallas_call(
        functools.partial(kernel, tiles_y, tiles_x),
        out_shape=(
            jax.ShapeDtypeStruct(base_prod.shape, F32),
            jax.ShapeDtypeStruct(resident.shape, F32),
        ),
        in_specs=[vmem] * 5 + [smem] * 4,
        out_specs=(vmem, vmem),
        scratch_shapes=[
            pltpu.VMEM((exchanges, SECTORS, ROWS + 2 * HALF, COLS), BF16),
            pltpu.VMEM((exchanges, 2, PAIRS2, ROWS, 128), BF16),
            pltpu.VMEM((exchanges, 2, PAIRS2, ROWS, 128), BF16),
            pltpu.VMEM((SECTORS, ROWS, COLS), BF16),
            pltpu.VMEM((SECTORS, ROWS, COLS), F32),
            pltpu.VMEM((SECTORS, ROWS, COLS), F32),
            pltpu.VMEM((2 * SECTORS, COLS), F32),
            pltpu.VMEM((2 * SECTORS, ROWS, COLS), BF16),
            pltpu.VMEM((2 * SECTORS, COLS, COLS), BF16),
            pltpu.VMEM((2 * SECTORS, COLS, COLS), BF16),
            pltpu.VMEM((GROUPS * ROWS, 128), BF16),
            pltpu.VMEM((far_pairs, GROUPS * ROWS), BF16),
            pltpu.VMEM((slots, far_pairs), BF16),
            pltpu.VMEM((GROUPS * ROWS, slots), BF16),
            pltpu.VMEM((GROUPS * ROWS, 128), F32),
            pltpu.VMEM((ITERS + 1, tiles_x, tiles_y * CAP, 128), BF16),
            pltpu.VMEM((ITERS + 1, tiles_x, tiles_y * CAP, 128), BF16),
            pltpu.VMEM((ITERS + 1, tiles_y, tiles_x * CAP, 128), BF16),
            pltpu.VMEM((ITERS + 1, tiles_y, tiles_x * CAP, 128), BF16),
            pltpu.VMEM((8, 128), F32),
            pltpu.VMEM((tiles_x, 8, 128), F32),
            pltpu.VMEM((8, 128), F32),
            pltpu.VMEM((tiles_y, 8, 128), F32),
            pltpu.VMEM((ROWS, COLS), F32),
            pltpu.VMEM((ITERS, ROWS, COLS), F32),
            dma((exchanges, 2)),
            dma((exchanges, 2, PAIRS2)),
            dma((exchanges, 2)),
            dma((exchanges, 2, PAIRS2)),
            dma((ITERS + 1,)),
            dma((ITERS + 1,)),
            dma((ITERS + 1,)),
            dma((ITERS + 1,)),
            dma((2,)),
            dma((2,)),
        ],
        compiler_params=pltpu.CompilerParams(
            collective_id=0, has_side_effects=True, vmem_limit_bytes=60 * 1024 * 1024
        ),
    )(
        base_prod,
        resident,
        floor_space,
        bracket,
        pairs,
        tax_rate,
        mixing,
        spill_decay,
        commute_decay,
    )


def solution(mesh):
    return jax.shard_map(
        body,
        mesh=mesh,
        in_specs=(
            P(None, "gy", "gx"),
            P("gy", "gx"),
            P("gy", "gx"),
            P("gy", "gx"),
            P(),
            P(),
            P(),
            P(),
            P(("gy", "gx"), None),
            P(("gy", "gx")),
            P(("gy", "gx")),
            P(("gy", "gx")),
        ),
        out_specs=(P(None, "gy", "gx"), P("gy", "gx")),
        check_vma=False,
    )
```

time: 677 us -> 128 us (0.19); the launches traced: 665 us -> 126 us
  local copies, waits for them, and re-layouts: 329 us -> 6.4 us
  starting transfers between devices: 123 us -> 0 us
  Pallas kernels: 0 us -> 119 us
  blocking collectives: 98.5 us -> 0 us
  waiting for transfers between devices: 45.1 us -> 0 us
  matrix products: 35 us -> 0 us
  other arithmetic: 28.7 us -> 0.05 us
    gather x4 -> x0, local copies, waits for them, and re-layouts: 242 us -> none  [tap_bands(): picked = tap_row[:, jnp.clip(tap_lag, 0, 2 * HALF)]]
    pallas_call x0 -> x1, Pallas kernels: none -> 119 us  [body(): pl.pallas_call(functools.partial(kernel, tiles_y, tiles_x), out_shape=(ja...]
    ppermute x24 -> x0, starting transfers between devices: 105 us -> none  [the longest x12 76.7 us: extended(): lax.ppermute(lax.slice_in_dim(block, 0, width, axis=dim), axis, backward)]
    psum x1 -> x0, blocking collectives: 65.3 us -> none  [body(): revenue = lax.psum(jnp.sum(resident * tax_cell * income), ('gy', 'gx'))]
    ppermute x24 -> x0, waiting for transfers between devices: 36.1 us -> none  [the longest x12 22.8 us: extended(): lax.ppermute(lax.slice_in_dim(block, block.shape[dim] - width, None, axis...]
    dot_general x34 -> x0, matrix products: 35 us -> none  [the longest x3 8.94 us: body(): jnp.dot(send_matrix, strip_table, preferred_element_type=jnp.float32)]
    all_to_all x2 -> x0, blocking collectives: 33.1 us -> none  [body(): lax.all_to_all(outgoing.reshape(devices, capacity, lane_width), ('gy', 'g...]
    convert_element_type x17 -> x0, local copies, waits for them, and re-layouts: 23.8 us -> none  [the longest x12 22.7 us: correlate(): tall_field = column_pass(padded, kernel_pair).astype(jnp.bfloat16)]
  transfers between devices with their start and end apart: 26 -> 0, of which waited for: 17 -> 0; matrix products, arithmetic and copies ran while one was open for 46% -> 0% of each run, Pallas kernels for 0% -> 0%
where the time goes in v1:
time: 128 us; the launch traced here: 126 us
  Pallas kernels  119 us (93%)
  local copies, waits for them, and re-layouts  6.4 us (5%)
    pallas_call x1, Pallas kernels, body(): pl.pallas_call(functools.partial(kernel, tiles_y, tiles_x), out_shape=(ja...  119 us
    unnamed x12, local copies, waits for them, and re-layouts  5.64 us

profile of v1, /device:TPU:24, one launch (start us, length us, event | category | flops | bytes accessed | tf_op | source)
XLA Modules:
  0.0 126.2 jit_solution(17805594447879898447)
XLA Ops:
  0.6 0.0 copy-start.4
  0.6 0.7 copy-done.4
  1.3 0.0 copy-start.1
  1.3 0.7 copy-done.1
  2.0 0.0 copy-start.3
  2.0 0.7 copy-done.3
  2.7 0.0 copy-start.2
  2.7 0.7 copy-done.2
  3.4 0.7 pad.4.pairs_ref
  4.1 119.1 %shard_map.131 = (f32[8,128,256]{2,1,0:T(8,128)}, f32[128,256]{1,0:T(8,128)}) custom-call(bf16[8,128,256]{2,1,0:T(8,128)(2,1)} %base_ref.1, f32[128,256]{1,0:T(8,128)} %resident_ref.1, f32[128,256]{1,0:T(8,128)} %floor_ref.1, s32[128,256]{1,0:T(8,128)} %bracket_ref.1, f32[128,512]{1,0:T(8,128)} %pad.4.pairs_ref, f32[8]{0:T(128)} %tax_ref.1, ...), custom_call_target="tpu_custom_call" | custom-call | tf_op jit(solution)/shard_map/pallas_call | solution.py:633
  123.2 0.0 copy-start
  123.2 2.3 %copy.16 = f32[8,128,256]{2,1,0:T(8,128)} copy(f32[8,128,256]{2,1,0:T(8,128)} %get-tuple-element.6) | data formatting | bytes 2097152
  125.5 0.0 copy-done
  125.5 0.7 copy.17
  (5 shorter events, 0.1 us)
Async XLA Ops:
  0.6 0.7 copy-start.4
  1.3 0.7 copy-start.1
  2.0 0.7 copy-start.3
  2.7 0.7 copy-start.2
  123.2 2.3 %copy-start = (f32[128,256]{1,0:T(8,128)S(1)}, f32[128,256]{1,0:T(8,128)}, u32[]{:S(2)}) copy-start(f32[128,256]{1,0:T(8,128)} %get-tuple-element.7) | copy-start | bytes 393220

commit v2 on v1

--- a/solution.py
+++ b/solution.py
@@ -18,24 +18,20 @@
 GROUPS = COLS // 16
 PAIRS2 = SECTORS // 2
 CHUNK = 16
+STEPS = HALF // CHUNK
 MESH = pl.DeviceIdType.MESH
 F32 = jnp.float32
 BF16 = jnp.bfloat16
 
 
 def swap_blocks(values):
-    values = list(values)
+    values = [pltpu.roll(v, 16 * s, 1) if s else v for s, v in enumerate(values)]
     block = lax.broadcasted_iota(jnp.int32, values[0].shape, 1) // 16
     for d in (1, 2, 4):
-        low = (block & d) == 0
-        for a in range(8):
-            if a & d:
-                continue
-            b = a + d
-            first, second = values[a], values[b]
-            values[a] = jnp.where(low, first, pltpu.roll(second, 16 * d, 1))
-            values[b] = jnp.where(low, pltpu.roll(first, 128 - 16 * d, 1), second)
-    return values
+        moved = (block & d) != 0
+        values = [jnp.where(moved, values[(a + d) % 8], values[a]) for a in range(8)]
+    values = [values[-g % 8] for g in range(8)]
+    return [pltpu.roll(v, 128 - 16 * g, 1) if g else v for g, v in enumerate(values)]
 
 
 def kernel(
@@ -46,11 +42,8 @@
     floor_ref,
     bracket_ref,
     pairs_ref,
-    tax_ref,
-    mixing_ref,
-    spill_ref,
-    commute_ref,
-    wage_ref,
+    scalar_ref,
+    power_ref,
     rent_ref,
     ext,
     edge_out,
@@ -112,31 +105,16 @@
     lax.fori_loop(1, tiles_x, greet_x, 0)
     lax.fori_loop(1, tiles_y, greet_y, 0)
 
-    @pl.when(my == 0)
-    def _():
-        ext[:, :, 0:HALF, :] = jnp.zeros((2 * ITERS, SECTORS, HALF, COLS), BF16)
-
-    @pl.when(my == tiles_y - 1)
-    def _():
-        ext[:, :, HALF + ROWS :, :] = jnp.zeros((2 * ITERS, SECTORS, HALF, COLS), BF16)
-
-    @pl.when(mx == 0)
-    def _():
-        edge_in[:, 0] = jnp.zeros((2 * ITERS, PAIRS2, ROWS, 128), BF16)
-
-    @pl.when(mx == tiles_x - 1)
-    def _():
-        edge_in[:, 1] = jnp.zeros((2 * ITERS, PAIRS2, ROWS, 128), BF16)
-
-    def row_copy(e, i, way):
+    def row_copy(e, j, way):
         start = HALF if way == 0 else ROWS
         land = HALF + ROWS if way == 0 else 0
         target = my - 1 if way == 0 else my + 1
-        return pltpu.make_async_remote_copy(
-            src_ref=ext.at[e, pl.ds(2 * i, 2), pl.ds(start, HALF), :],
-            dst_ref=ext.at[e, pl.ds(2 * i, 2), pl.ds(land, HALF), :],
+        step = pl.multiple_of(j * CHUNK, CHUNK)
+        return pltpu.make_async_remote_copy(
+            src_ref=ext.at[e, :, pl.ds(start + step, CHUNK), :],
+            dst_ref=ext.at[e, :, pl.ds(land + step, CHUNK), :],
             send_sem=row_send.at[e, way],
-            recv_sem=row_recv.at[e, way, i],
+            recv_sem=row_recv.at[e, way, j],
             device_id=(target, mx),
             device_id_type=MESH,
         )
@@ -156,17 +134,26 @@
     can_row = (my > 0, my < tiles_y - 1)
     can_edge = (mx > 0, mx < tiles_x - 1)
 
-    def send_rows(e, way):
-        @pl.when(can_row[way])
-        def _():
-            for i in range(PAIRS2):
-                row_copy(e, i, way).start()
+    def send_rows(e, j):
+        for way in range(2):
+
+            @pl.when(can_row[way])
+            def _():
+                row_copy(e, j, way).start()
+
+    def wait_rows(e):
+        for way in range(2):
+
+            @pl.when(can_row[1 - way])
+            def _():
+                for j in range(STEPS):
+                    row_copy(e, j, way).wait_recv()
 
     def edge_copy(e, i, way):
         target = mx - 1 if way == 0 else mx + 1
         return pltpu.make_async_remote_copy(
-            src_ref=edge_out.at[e, way, i],
-            dst_ref=edge_in.at[e, 1 - way, i],
+            src_ref=edge_out.at[e, way, pl.ds(2 * i, 2)],
+            dst_ref=edge_in.at[e, 1 - way, pl.ds(2 * i, 2)],
             send_sem=edge_send.at[e, way],
             recv_sem=edge_recv.at[e, way, i],
             device_id=(my, target),
@@ -187,49 +174,47 @@
     lane128 = lax.broadcasted_iota(jnp.int32, (ROWS, 128), 1)
 
     def rows_pass(e, kind):
-        def one(i, carry):
-            for way in range(2):
-
-                @pl.when(can_row[1 - way])
-                def _():
-                    row_copy(e, i, way).wait_recv()
-
-            ends = []
+        wait_rows(e)
+
+        def one(half, carry):
             for k in range(2):
-                s = 2 * i + k
-                passed = jnp.dot(
-                    band_row[kind * SECTORS + s], ext[e, s], preferred_element_type=F32
-                )
-                mid[s] = passed.astype(BF16)
-                ends.append((passed[:, 0:128], passed[:, 128:256]))
-            first, second = ends
-            low = lane128 < HALF
-            edge_out[e, 0, i] = jnp.where(low, first[0], pltpu.roll(second[0], HALF, 1)).astype(
-                BF16
-            )
-            edge_out[e, 1, i] = jnp.where(low, pltpu.roll(second[1], HALF, 1), first[1]).astype(
-                BF16
-            )
+                i = 2 * half + k
+                ends = []
+                for s in (2 * i, 2 * i + 1):
+                    passed = jnp.dot(
+                        band_row[kind * SECTORS + s], ext[e, s], preferred_element_type=F32
+                    )
+                    mid[s] = passed.astype(BF16)
+                    ends.append((passed[:, 0:128], passed[:, 128:256]))
+                first, second = ends
+                low = lane128 < HALF
+                edge_out[e, 0, i] = jnp.where(
+                    low, first[0], pltpu.roll(second[0], HALF, 1)
+                ).astype(BF16)
+                edge_out[e, 1, i] = jnp.where(
+                    low, pltpu.roll(second[1], HALF, 1), first[1]
+                ).astype(BF16)
             for way in range(2):
 
                 @pl.when(can_edge[way])
                 def _():
-                    edge_copy(e, i, way).start()
+                    edge_copy(e, half, way).start()
 
             return carry
 
-        lax.fori_loop(0, PAIRS2, one, 0)
+        lax.fori_loop(0, 2, one, 0)
 
     def columns_pass(e, kind, result):
-        def one(i, carry):
+        def one(half, carry):
             for way in range(2):
 
                 @pl.when(can_edge[1 - way])
                 def _():
-                    edge_copy(e, i, way).wait_recv()
-
-            for k in range(2):
-                s = 2 * i + k
+                    edge_copy(e, half, way).wait_recv()
+
+            for k in range(4):
+                s = 4 * half + k
+                i = 2 * half + k // 2
                 b = kind * SECTORS + s
                 value = jnp.dot(mid[s], band_col[b], preferred_element_type=F32)
                 value += jnp.dot(
@@ -241,7 +226,7 @@
                 result[s] = value
             return carry
 
-        lax.fori_loop(0, PAIRS2, one, 0)
+        lax.fori_loop(0, 2, one, 0)
 
     def make_bands(kind):
         u = lax.broadcasted_iota(jnp.int32, (COLS, COLS), 0)
@@ -372,9 +357,30 @@
             device_id_type=MESH,
         )
 
+    def unit(r, h):
+        return pl.ds(r, CHUNK), pl.ds(pl.multiple_of(128 * h, 128), 128)
+
+    def strip_rows(r, h, g):
+        return pl.ds(pl.multiple_of((8 * h + g) * ROWS + r, CHUNK), CHUNK)
+
+    def over_cells(work, sent, carry, wide):
+        def step(j, carry):
+            def one(u, carry):
+                for k in range(wide):
+                    number = u * wide + k
+                    r = pl.multiple_of((number // 2) * HALF + j * CHUNK, CHUNK)
+                    carry = work(r, number % 2, carry)
+                return carry
+
+            carry = one(0, carry) if wide == 4 else lax.fori_loop(0, 4 // wide, one, carry)
+            if sent is not None:
+                send_rows(sent, j)
+            return carry
+
+        return lax.fori_loop(0, STEPS, step, carry)
+
     def shares(it, r, h, wages, revenue):
-        rows = pl.ds(r, CHUNK)
-        lanes = slice(128 * h, 128 * h + 128)
+        rows, lanes = unit(r, h)
         powers = [w * w * w for w in wages]
         inverse = 1.0 / sum(powers[1:], powers[0])
         people = resident_ref[rows, lanes]
@@ -385,7 +391,7 @@
         for s in range(SECTORS):
             ext[2 * it, s, pl.ds(HALF + r, CHUNK), lanes] = supply[s].astype(BF16)
         for g, strip in enumerate(swap_blocks(supply)):
-            table[pl.ds((8 * h + g) * ROWS + r, CHUNK), :] = strip.astype(BF16)
+            table[strip_rows(r, h, g), :] = strip.astype(BF16)
         gain = people * rate_ref[rows, lanes] * income
         return revenue + gain[0:8] + gain[8:16]
 
@@ -396,27 +402,21 @@
 
     zero = jnp.zeros((8, 128), F32)
 
-    def first_chunk(c, carry):
+    def first_cells(r, h, carry):
         people_sum, revenue = carry
-        r = pl.multiple_of(c * CHUNK, CHUNK)
-        rows = pl.ds(r, CHUNK)
-        for h in range(2):
-            lanes = slice(128 * h, 128 * h + 128)
-            bracket = bracket_ref[rows, lanes]
-            rate = jnp.zeros((CHUNK, 128), F32)
-            for b in range(8):
-                rate = jnp.where(bracket == b, tax_ref[b], rate)
-            rate_ref[rows, lanes] = rate
-            people = resident_ref[rows, lanes]
-            people_sum = people_sum + people[0:8] + people[8:16]
-            wages = [base_ref[s, rows, lanes].astype(F32) for s in range(SECTORS)]
-            revenue = shares(0, r, h, wages, revenue)
-        return people_sum, revenue
-
-    people_sum, revenue0 = lax.fori_loop(0, ROWS // CHUNK, first_chunk, (zero, zero))
+        rows, lanes = unit(r, h)
+        bracket = bracket_ref[rows, lanes]
+        rate = jnp.zeros((CHUNK, 128), F32)
+        for b in range(8):
+            rate = jnp.where(bracket == b, scalar_ref[b], rate)
+        rate_ref[rows, lanes] = rate
+        people = resident_ref[rows, lanes]
+        people_sum = people_sum + people[0:8] + people[8:16]
+        wages = [base_ref[s, rows, lanes].astype(F32) for s in range(SECTORS)]
+        return people_sum, shares(0, r, h, wages, revenue)
+
     pl.semaphore_wait(barrier, tiles_x - 1 + tiles_y - 1)
-    send_rows(0, 0)
-    send_rows(0, 1)
+    people_sum, revenue0 = over_cells(first_cells, 0, (zero, zero), 4)
 
     across = pairs_ref[...].T
     dest_row, slot_base = pairs_ref[0:1, :], pairs_ref[1:2, :]
@@ -441,12 +441,28 @@
     gather(0)
     start_first(0)
 
+    @pl.when(my == 0)
+    def _():
+        ext[:, :, 0:HALF, :] = jnp.zeros((2 * ITERS, SECTORS, HALF, COLS), BF16)
+
+    @pl.when(my == tiles_y - 1)
+    def _():
+        ext[:, :, HALF + ROWS :, :] = jnp.zeros((2 * ITERS, SECTORS, HALF, COLS), BF16)
+
+    @pl.when(mx == 0)
+    def _():
+        edge_in[:, 0] = jnp.zeros((2 * ITERS, PAIRS2, ROWS, 128), BF16)
+
+    @pl.when(mx == tiles_x - 1)
+    def _():
+        edge_in[:, 1] = jnp.zeros((2 * ITERS, PAIRS2, ROWS, 128), BF16)
+
     sector = lax.broadcasted_iota(jnp.int32, (2 * SECTORS, COLS), 0)
     tap = lax.broadcasted_iota(jnp.int32, (2 * SECTORS, COLS), 1)
     decay = jnp.zeros((2 * SECTORS, COLS), F32)
     for s in range(SECTORS):
-        decay = jnp.where(sector == s, commute_ref[s], decay)
-        decay = jnp.where(sector == SECTORS + s, spill_ref[s], decay)
+        decay = jnp.where(sector == s, scalar_ref[8 + s], decay)
+        decay = jnp.where(sector == SECTORS + s, scalar_ref[16 + s], decay)
     offset = jnp.abs(tap - HALF).astype(F32) / HALF
     unscaled = jnp.where(tap <= 2 * HALF, jnp.exp(-decay * offset), 0.0)
     tap_row[...] = (unscaled / jnp.sum(unscaled, axis=1, keepdims=True)).astype(BF16).astype(F32)
@@ -479,8 +495,6 @@
     revenues = [revenue0]
     for it in range(ITERS):
         if it > 0:
-            send_rows(2 * it, 0)
-            send_rows(2 * it, 1)
             gather(it)
             start_first(it)
         if it == ITERS - 1:
@@ -517,21 +531,16 @@
             place[...], two_in[it].reshape(slots, 128), preferred_element_type=F32
         )
 
-        def labor_chunk(c, carry):
-            r = pl.multiple_of(c * CHUNK, CHUNK)
-            for h in range(2):
-                lanes = slice(128 * h, 128 * h + 128)
-                strips = [far[pl.ds((8 * h + g) * ROWS + r, CHUNK), :] for g in range(8)]
-                for s, flow in enumerate(swap_blocks(strips)):
-                    value = near[s, pl.ds(r, CHUNK), lanes] + FAR_SCALE * flow
-                    labor[s, pl.ds(r, CHUNK), lanes] = value
-                    ext[2 * it + 1, s, pl.ds(HALF + r, CHUNK), lanes] = value.astype(BF16)
+        def labor_cells(r, h, carry):
+            rows, lanes = unit(r, h)
+            strips = [far[strip_rows(r, h, g), :] for g in range(8)]
+            for s, flow in enumerate(swap_blocks(strips)):
+                value = near[s, rows, lanes] + FAR_SCALE * flow
+                labor[s, rows, lanes] = value
+                ext[2 * it + 1, s, pl.ds(HALF + r, CHUNK), lanes] = value.astype(BF16)
             return carry
 
-        lax.fori_loop(0, HALF // CHUNK, labor_chunk, 0)
-        send_rows(2 * it + 1, 0)
-        lax.fori_loop(HALF // CHUNK, ROWS // CHUNK, labor_chunk, 0)
-        send_rows(2 * it + 1, 1)
+        over_cells(labor_cells, 2 * it + 1, 0, 4)
         if it == 0:
             make_bands(1)
         if it == ITERS - 1:
@@ -544,38 +553,37 @@
                 rows = pl.ds(pl.multiple_of(c * CHUNK, CHUNK), CHUNK)
                 keep = 1.0 - rate_ref[rows, :]
                 people, space = resident_ref[rows, :], floor_ref[rows, :]
-                rent = None
+                ratio = people / space
+                square = None
                 for k in range(ITERS):
                     net = keep * income_ref[k, rows, :] + transfers[k]
-                    level = people if rent is None else rent * people
-                    rent = jnp.sqrt(level * net / space)
-                rent_ref[rows, :] = rent
+                    level = ratio if square is None else jnp.sqrt(square) * ratio
+                    square = level * net
+                rent_ref[rows, :] = square
                 return carry
 
             lax.fori_loop(0, ROWS // CHUNK, rent_chunk, 0)
         rows_pass(2 * it + 1, 1)
         columns_pass(2 * it + 1, 1, near)
 
-        def wage_chunk(c, revenue):
-            r = pl.multiple_of(c * CHUNK, CHUNK)
-            rows = pl.ds(r, CHUNK)
-            for h in range(2):
-                lanes = slice(128 * h, 128 * h + 128)
-                logs = [jnp.log(1.0 + near[s, rows, lanes]) for s in range(SECTORS)]
-                wages = []
-                for s in range(SECTORS):
-                    power = -BETA_WAGE * jnp.log(1.0 + labor[s, rows, lanes])
-                    for t in range(SECTORS):
-                        power = power + mixing_ref[s, t] * logs[t]
+        def wage_cells(r, h, revenue):
+            rows, lanes = unit(r, h)
+            logs = [jnp.log(1.0 + near[s, rows, lanes]) for s in range(SECTORS)]
+            wages = []
+            for s in range(SECTORS):
+                power = -BETA_WAGE * jnp.log(1.0 + labor[s, rows, lanes])
+                for t in range(SECTORS):
+                    power = power + scalar_ref[24 + SECTORS * s + t] * logs[t]
+                if it == ITERS - 1:
+                    power_ref[s, rows, lanes] = power
+                else:
                     wages.append(base_ref[s, rows, lanes].astype(F32) * jnp.exp(power))
-                if it == ITERS - 1:
-                    for s in range(SECTORS):
-                        wage_ref[s, rows, lanes] = wages[s]
-                else:
-                    revenue = shares(it + 1, r, h, wages, revenue)
+            if it < ITERS - 1:
+                revenue = shares(it + 1, r, h, wages, revenue)
             return revenue
 
-        revenues.append(lax.fori_loop(0, ROWS // CHUNK, wage_chunk, zero))
+        sent = 2 * it + 2 if it < ITERS - 1 else None
+        revenues.append(over_cells(wage_cells, sent, zero, 2))
 
     for e in range(2 * ITERS):
         for way in range(2):
@@ -630,13 +638,14 @@
     smem = pl.BlockSpec(memory_space=pltpu.SMEM)
     exchanges = 2 * ITERS
     dma = pltpu.SemaphoreType.DMA
-    return pl.pallas_call(
+    scalars = jnp.concatenate([tax_rate, commute_decay, spill_decay, mixing.reshape(-1)])
+    power, square = pl.pallas_call(
         functools.partial(kernel, tiles_y, tiles_x),
         out_shape=(
             jax.ShapeDtypeStruct(base_prod.shape, F32),
             jax.ShapeDtypeStruct(resident.shape, F32),
         ),
-        in_specs=[vmem] * 5 + [smem] * 4,
+        in_specs=[vmem] * 5 + [smem],
         out_specs=(vmem, vmem),
         scratch_shapes=[
             pltpu.VMEM((exchanges, SECTORS, ROWS + 2 * HALF, COLS), BF16),
@@ -665,9 +674,9 @@
             pltpu.VMEM((ROWS, COLS), F32),
             pltpu.VMEM((ITERS, ROWS, COLS), F32),
             dma((exchanges, 2)),
-            dma((exchanges, 2, PAIRS2)),
+            dma((exchanges, 2, STEPS)),
             dma((exchanges, 2)),
-            dma((exchanges, 2, PAIRS2)),
+            dma((exchanges, 2, 2)),
             dma((ITERS + 1,)),
             dma((ITERS + 1,)),
             dma((ITERS + 1,)),
@@ -684,11 +693,9 @@
         floor_space,
         bracket,
         pairs,
-        tax_rate,
-        mixing,
-        spill_decay,
-        commute_decay,
+        scalars,
     )
+    return base_prod.astype(F32) * jnp.exp(power), jnp.sqrt(square)
 
 
 def solution(mesh):

time: 128 us -> 121 us (0.945); the launches traced: 126 us -> 121 us
  Pallas kernels: 119 us -> 113 us
  other arithmetic: 0.05 us -> 3.02 us
  local copies, waits for them, and re-layouts: 6.4 us -> 4.34 us
    pallas_call x1, Pallas kernels: 119 us -> 113 us  [body(): pl.pallas_call(functools.partial(kernel, tiles_y, tiles_x), out_shape=(ja...]
    unnamed x12 -> x18, local copies, waits for them, and re-layouts: 5.64 us -> 2.11 us
    mul x0 -> x1, other arithmetic: none -> 2.38 us  [body(): return (base_prod.astype(F32) * jnp.exp(power), jnp.sqrt(square))]
where the time goes in v2:
time: 121 us
  Pallas kernels  113 us (93%)
  local copies, waits for them, and re-layouts  4.34 us (4%)
  other arithmetic  3.02 us (2%)
    pallas_call x1, Pallas kernels, body(): pl.pallas_call(functools.partial(kernel, tiles_y, tiles_x), out_shape=(ja...  113 us

profile of v2, /device:TPU:24, one launch (start us, length us, event | category | flops | bytes accessed | tf_op | source)
XLA Modules:
  0.0 120.7 jit_solution(7238917573964436181)
XLA Ops:
  0.6 0.0 copy-start.6
  0.6 0.0 copy-start.7
  0.7 0.0 copy-start.8
  0.7 0.8 reshape.111
  1.4 0.0 copy-done.6
  1.4 0.0 copy-done.7
  1.5 0.0 copy-done.8
  1.5 0.0 copy-start.5
  1.5 0.6 pad_maximum_fusion.scalar_ref
  2.1 0.1 copy-done.5
  2.2 0.0 copy-start.2
  2.2 0.7 copy-done.2
  2.8 0.0 copy-start.4
  2.9 0.7 copy-done.4
  3.5 0.0 copy-start.3
  3.5 0.7 copy-done.3
  4.3 0.7 pad.4.pairs_ref
  5.0 0.0 copy-start
  5.0 112.6 %shard_map.131 = (f32[8,128,256]{2,1,0:T(8,128)}, f32[128,256]{1,0:T(8,128)}) custom-call(bf16[8,128,256]{2,1,0:T(8,128)(2,1)} %base_ref.1, f32[128,256]{1,0:T(8,128)} %resident_ref.1, f32[128,256]{1,0:T(8,128)} %floor_ref.1, s32[128,256]{1,0:T(8,128)} %bracket_ref.1, f32[128,512]{1,0:T(8,128)} %pad.4.pairs_ref, f32[88]{0:T(128)} %pad_maximum_fusion.scalar_ref), custom_call_target="tpu_custom_call" | custom-call | tf_op jit(solution)/shard_map/pallas_call | solution.py:642
  117.6 0.0 copy-done
  117.6 0.0 copy-start.1
  117.6 2.4 %exponential_multiply_fusion = f32[8,128,256]{2,1,0:T(8,128)} fusion(f32[8,128,256]{2,1,0:T(8,128)} %get-tuple-element.4, bf16[8,128,256]{2,1,0:T(8,128)(2,1)S(1)} %copy-done), kind=kLoop, calls=%fused_computation | loop fusion | flops 524288 | bytes 2621440 | tf_op jit(solution)/shard_map/mul | solution.py:698
  120.0 0.0 copy-done.1
  120.0 0.7 sqrt.3
  (5 shorter events, 0.1 us)
Async XLA Ops:
  0.6 0.8 copy-start.6
  0.6 0.8 copy-start.7
  0.7 0.8 copy-start.8
  1.5 0.7 copy-start.5
  2.2 0.7 copy-start.2
  2.8 0.7 copy-start.4
  3.5 0.7 copy-start.3
  5.0 112.6 %copy-start = (bf16[8,128,256]{2,1,0:T(8,128)(2,1)S(1)}, bf16[8,128,256]{2,1,0:T(8,128)(2,1)}, u32[]{:S(2)}) copy-start(bf16[8,128,256]{2,1,0:T(8,128)(2,1)} %base_ref.1) | copy-start | bytes 1572868
  117.6 2.4 %copy-start.1 = (f32[128,256]{1,0:T(8,128)S(1)}, f32[128,256]{1,0:T(8,128)}, u32[]{:S(2)}) copy-start(f32[128,256]{1,0:T(8,128)} %get-tuple-element.5) | copy-start | bytes 393220

commit v3 on v2

--- a/solution.py
+++ b/solution.py
@@ -41,8 +41,14 @@
     resident_ref,
     floor_ref,
     bracket_ref,
-    pairs_ref,
-    scalar_ref,
+    dest_ref,
+    src_ref,
+    dst_ref,
+    count_ref,
+    tax_any,
+    commute_any,
+    spill_any,
+    mixing_any,
     power_ref,
     rent_ref,
     ext,
@@ -70,6 +76,12 @@
     total_in,
     rate_ref,
     income_ref,
+    last_in,
+    tax_ref,
+    commute_ref,
+    spill_ref,
+    mixing_ref,
+    load_sem,
     row_send,
     row_recv,
     edge_send,
@@ -83,27 +95,46 @@
 ):
     my = lax.axis_index("gy")
     mx = lax.axis_index("gx")
-    slots_x = tiles_y * CAP
-    slots_y = tiles_x * CAP
-    slots = tiles_x * slots_x
-    far_pairs = pairs_ref.shape[1]
+    chips_x = tiles_x // 2
+    chips = tiles_y * chips_x
+    core = lax.rem(mx, 2)
+    chip_x = mx // 2
+    sibling = mx + 1 - 2 * core
+    beyond = lax.rem(mx + 2 * core - 1 + tiles_x, tiles_x)
+    mine = my * chips_x + chip_x
+    slots = tiles_y * tiles_x * CAP
+    far_pairs = dest_ref.shape[1]
+
+    loads = [
+        pltpu.make_async_copy(source, target, load_sem.at[k])
+        for k, (source, target) in enumerate(
+            (
+                (tax_any, tax_ref),
+                (commute_any, commute_ref),
+                (spill_any, spill_ref),
+                (mixing_any, mixing_ref),
+            )
+        )
+    ]
+    for load in loads:
+        load.start()
 
     barrier = pltpu.get_barrier_semaphore()
 
-    def greet_x(j, carry):
-        pl.semaphore_signal(
-            barrier, inc=1, device_id=(my, lax.rem(mx + j, tiles_x)), device_id_type=MESH
-        )
+    def chip_at(j):
+        return lax.rem(my + j // chips_x, tiles_y), lax.rem(chip_x + lax.rem(j, chips_x), chips_x)
+
+    def greet(y, x):
+        pl.semaphore_signal(barrier, inc=1, device_id=(y, x), device_id_type=MESH)
+
+    def greet_chip(j, carry):
+        y, x = chip_at(j)
+        greet(y, 2 * x + core)
         return carry
 
-    def greet_y(j, carry):
-        pl.semaphore_signal(
-            barrier, inc=1, device_id=(lax.rem(my + j, tiles_y), mx), device_id_type=MESH
-        )
-        return carry
-
-    lax.fori_loop(1, tiles_x, greet_x, 0)
-    lax.fori_loop(1, tiles_y, greet_y, 0)
+    greet(my, sibling)
+    greet(my, beyond)
+    lax.fori_loop(1, chips, greet_chip, 0)
 
     def row_copy(e, j, way):
         start = HALF if way == 0 else ROWS
@@ -252,78 +283,59 @@
 
         lax.fori_loop(0, SECTORS, one, 0)
 
-    def first_copy(a, x):
-        return pltpu.make_async_remote_copy(
-            src_ref=one_out.at[a, x],
-            dst_ref=one_in.at[a, mx],
+    def first_copy(a, y, x):
+        return pltpu.make_async_remote_copy(
+            src_ref=one_out.at[a, y * chips_x + x],
+            dst_ref=one_in.at[a, mine],
             send_sem=one_send.at[a],
             recv_sem=one_recv.at[a],
-            device_id=(my, x),
+            device_id=(y, 2 * x + core),
             device_id_type=MESH,
         )
 
     def first_all(a):
         return pltpu.make_async_remote_copy(
-            src_ref=one_out.at[a, pl.ds(0, tiles_x - 1)],
-            dst_ref=one_in.at[a, pl.ds(0, tiles_x - 1)],
+            src_ref=one_out.at[a, pl.ds(0, chips - 1)],
+            dst_ref=one_in.at[a, pl.ds(0, chips - 1)],
             send_sem=one_send.at[a],
             recv_sem=one_recv.at[a],
-            device_id=(my, lax.rem(mx + 1, tiles_x)),
-            device_id_type=MESH,
-        )
-
-    def second_copy(a, y):
-        return pltpu.make_async_remote_copy(
-            src_ref=two_out.at[a, y],
-            dst_ref=two_in.at[a, my],
+            device_id=(my, sibling),
+            device_id_type=MESH,
+        )
+
+    def second_copy(a):
+        return pltpu.make_async_remote_copy(
+            src_ref=two_out.at[a],
+            dst_ref=two_in.at[a, 1],
             send_sem=two_send.at[a],
             recv_sem=two_recv.at[a],
-            device_id=(y, mx),
-            device_id_type=MESH,
-        )
-
-    def second_all(a):
-        return pltpu.make_async_remote_copy(
-            src_ref=two_out.at[a, pl.ds(0, tiles_y - 1)],
-            dst_ref=two_in.at[a, pl.ds(0, tiles_y - 1)],
-            send_sem=two_send.at[a],
-            recv_sem=two_recv.at[a],
-            device_id=(lax.rem(my + 1, tiles_y), mx),
+            device_id=(my, sibling),
             device_id_type=MESH,
         )
 
     def start_first(a):
         def one(j, carry):
-            first_copy(a, lax.rem(mx + j, tiles_x)).start()
+            first_copy(a, *chip_at(j)).start()
             return carry
 
-        lax.fori_loop(1, tiles_x, one, 0)
-        one_in[a, mx] = one_out[a, mx]
+        lax.fori_loop(1, chips, one, 0)
+        one_in[a, mine] = one_out[a, mine]
 
     def pass_on(a):
         first_all(a).wait_recv()
-        for i in range(tiles_x // 2):
-            pieces = [
-                one_in[a, 2 * i + k].astype(F32).reshape(tiles_y, CAP, 128) for k in range(2)
-            ]
-            two_out[a, :, 2 * i * CAP : 2 * (i + 1) * CAP, :] = jnp.concatenate(
-                pieces, axis=1
-            ).astype(BF16)
-
-        def one(j, carry):
-            second_copy(a, lax.rem(my + j, tiles_y)).start()
-            return carry
-
-        lax.fori_loop(1, tiles_y, one, 0)
-        two_in[a, my] = two_out[a, my]
+        parts = one_in[a].astype(F32).reshape(chips, 2, CAP, 128)
+        low, high = parts[:, 0], parts[:, 1]
+        two_out[a] = jnp.where(core == 0, high, low).reshape(chips * CAP, 128).astype(BF16)
+        second_copy(a).start()
+        two_in[a, 0] = jnp.where(core == 0, low, high).reshape(chips * CAP, 128).astype(BF16)
 
     def sum_copy(x):
         return pltpu.make_async_remote_copy(
             src_ref=sum_out,
-            dst_ref=sum_in.at[mx],
+            dst_ref=sum_in.at[chip_x],
             send_sem=sum_send.at[0],
             recv_sem=sum_recv.at[0],
-            device_id=(my, x),
+            device_id=(my, 2 * x + core),
             device_id_type=MESH,
         )
 
@@ -339,11 +351,11 @@
 
     def sum_all():
         return pltpu.make_async_remote_copy(
-            src_ref=sum_in.at[pl.ds(0, tiles_x - 1)],
-            dst_ref=sum_in.at[pl.ds(0, tiles_x - 1)],
+            src_ref=sum_in.at[pl.ds(0, chips_x - 1)],
+            dst_ref=sum_in.at[pl.ds(0, chips_x - 1)],
             send_sem=sum_send.at[0],
             recv_sem=sum_recv.at[0],
-            device_id=(my, lax.rem(mx + 1, tiles_x)),
+            device_id=(my, sibling),
             device_id_type=MESH,
         )
 
@@ -353,7 +365,17 @@
             dst_ref=total_in.at[pl.ds(0, tiles_y - 1)],
             send_sem=sum_send.at[1],
             recv_sem=sum_recv.at[1],
-            device_id=(lax.rem(my + 1, tiles_y), mx),
+            device_id=(my, sibling),
+            device_id_type=MESH,
+        )
+
+    def last_copy():
+        return pltpu.make_async_remote_copy(
+            src_ref=last_in.at[0],
+            dst_ref=last_in.at[1],
+            send_sem=sum_send.at[2],
+            recv_sem=sum_recv.at[2],
+            device_id=(my, sibling),
             device_id_type=MESH,
         )
 
@@ -398,7 +420,7 @@
     def gather(a):
         picked = jnp.dot(source_hot[...], table[...], preferred_element_type=F32).astype(BF16)
         ordered = jnp.dot(slot_hot[...], picked, preferred_element_type=F32).astype(BF16)
-        one_out[a] = ordered.reshape(tiles_x, slots_x, 128)
+        one_out[a] = ordered.reshape(chips, 2 * CAP, 128)
 
     zero = jnp.zeros((8, 128), F32)
 
@@ -408,34 +430,52 @@
         bracket = bracket_ref[rows, lanes]
         rate = jnp.zeros((CHUNK, 128), F32)
         for b in range(8):
-            rate = jnp.where(bracket == b, scalar_ref[b], rate)
+            rate = jnp.where(bracket == b, tax_ref[b], rate)
         rate_ref[rows, lanes] = rate
         people = resident_ref[rows, lanes]
         people_sum = people_sum + people[0:8] + people[8:16]
         wages = [base_ref[s, rows, lanes].astype(F32) for s in range(SECTORS)]
         return people_sum, shares(0, r, h, wages, revenue)
 
-    pl.semaphore_wait(barrier, tiles_x - 1 + tiles_y - 1)
-    people_sum, revenue0 = over_cells(first_cells, 0, (zero, zero), 4)
-
-    across = pairs_ref[...].T
-    dest_row, slot_base = pairs_ref[0:1, :], pairs_ref[1:2, :]
+    for load in loads:
+        load.wait()
+    people_sum, revenue0 = over_cells(first_cells, None, (zero, zero), 4)
+    pl.semaphore_wait(barrier, chips + 1)
+    for j in range(STEPS):
+        send_rows(0, j)
+
+    line = lax.broadcasted_iota(jnp.int32, (8, far_pairs), 0)
+    source, target = src_ref[...], dst_ref[...]
+    row, group = target >> 4, target & 15
+    fields = [
+        dest_ref[...],
+        (source & 15) * ROWS + (source >> 4),
+        ((((row >> 4) & 3) * 2 + (row >> 6)) * GROUPS) + group,
+        row & 15,
+        count_ref[...],
+    ]
+    pairs = jnp.zeros((8, far_pairs), jnp.int32)
+    for k, field in enumerate(fields):
+        pairs = jnp.where(line == k, field, pairs)
+    pairs = pairs.astype(F32)
+    across = jnp.concatenate([pairs, jnp.zeros((120, far_pairs), F32)], axis=0).T
+    dest_row = pairs[0:1, :]
     earlier = lax.broadcasted_iota(jnp.int32, (far_pairs, far_pairs), 0) < (
         lax.broadcasted_iota(jnp.int32, (far_pairs, far_pairs), 1)
     )
     same = (across[:, 0:1] == dest_row) & earlier
     rank = jnp.sum(jnp.where(same, 1.0, 0.0), axis=0, keepdims=True)
-    slot_of = (slot_base + rank).astype(jnp.int32)
+    slot_of = (dest_row * CAP + rank).astype(jnp.int32)
     slot_ids = lax.broadcasted_iota(jnp.int32, (slots, far_pairs), 0)
     slot_hot[...] = jnp.where(slot_ids == slot_of, 1.0, 0.0).astype(BF16)
     strip_ids = lax.broadcasted_iota(jnp.int32, (far_pairs, GROUPS * ROWS), 1)
     source_hot[...] = jnp.where(
-        strip_ids == across[:, 2:3].astype(jnp.int32), 1.0, 0.0
+        strip_ids == across[:, 1:2].astype(jnp.int32), 1.0, 0.0
     ).astype(BF16)
     one_out[ITERS] = (
         jnp.dot(slot_hot[...], across.astype(BF16), preferred_element_type=F32)
         .astype(BF16)
-        .reshape(tiles_x, slots_x, 128)
+        .reshape(chips, 2 * CAP, 128)
     )
     start_first(ITERS)
     gather(0)
@@ -461,8 +501,8 @@
     tap = lax.broadcasted_iota(jnp.int32, (2 * SECTORS, COLS), 1)
     decay = jnp.zeros((2 * SECTORS, COLS), F32)
     for s in range(SECTORS):
-        decay = jnp.where(sector == s, scalar_ref[8 + s], decay)
-        decay = jnp.where(sector == SECTORS + s, scalar_ref[16 + s], decay)
+        decay = jnp.where(sector == s, commute_ref[s], decay)
+        decay = jnp.where(sector == SECTORS + s, spill_ref[s], decay)
     offset = jnp.abs(tap - HALF).astype(F32) / HALF
     unscaled = jnp.where(tap <= 2 * HALF, jnp.exp(-decay * offset), 0.0)
     tap_row[...] = (unscaled / jnp.sum(unscaled, axis=1, keepdims=True)).astype(BF16).astype(F32)
@@ -471,13 +511,13 @@
     pass_on(ITERS)
 
     def build_place():
-        second_all(ITERS).wait_recv()
+        second_copy(ITERS).wait_recv()
         routing = two_in[ITERS].reshape(slots, 128)
         line = lax.broadcasted_iota(jnp.int32, (16, 128), 0)
         lane = lax.broadcasted_iota(jnp.int32, (16, 128), 1)
-        pick = jnp.where((line == 0) & (lane == 3), 1.0, 0.0)
-        pick = jnp.where((line == 0) & (lane == 4), float(ROWS), pick)
-        pick = jnp.where((line == 1) & (lane == 5), 1.0, pick).astype(BF16)
+        pick = jnp.where((line == 0) & (lane == 2), float(CHUNK), 0.0)
+        pick = jnp.where((line == 0) & (lane == 3), 1.0, pick)
+        pick = jnp.where((line == 1) & (lane == 4), 1.0, pick).astype(BF16)
         found = lax.dot_general(
             pick, routing, (((1,), (1,)), ((), ())), preferred_element_type=F32
         )
@@ -505,11 +545,11 @@
             sum_out[...] = parts
 
             def start_sum(j, carry):
-                sum_copy(lax.rem(mx + j, tiles_x)).start()
+                sum_copy(lax.rem(chip_x + j, chips_x)).start()
                 return carry
 
-            lax.fori_loop(1, tiles_x, start_sum, 0)
-            sum_in[mx] = parts
+            lax.fori_loop(1, chips_x, start_sum, 0)
+            sum_in[chip_x] = parts
         rows_pass(2 * it, 0)
         pass_on(it)
         if it == ITERS - 1:
@@ -524,28 +564,40 @@
             lax.fori_loop(1, tiles_y, start_total, 0)
             total_in[my] = halfway
         columns_pass(2 * it, 0, near)
+        if it == ITERS - 1:
+            total_all().wait_recv()
+            last_in[0] = jnp.sum(total_in[...], axis=0)
+            last_copy().start()
         if it == 0:
             build_place()
-        second_all(it).wait_recv()
-        far[...] = jnp.dot(
-            place[...], two_in[it].reshape(slots, 128), preferred_element_type=F32
-        )
-
-        def labor_cells(r, h, carry):
-            rows, lanes = unit(r, h)
-            strips = [far[strip_rows(r, h, g), :] for g in range(8)]
-            for s, flow in enumerate(swap_blocks(strips)):
-                value = near[s, rows, lanes] + FAR_SCALE * flow
-                labor[s, rows, lanes] = value
-                ext[2 * it + 1, s, pl.ds(HALF + r, CHUNK), lanes] = value.astype(BF16)
+        second_copy(it).wait_recv()
+
+        def labor_step(j, carry):
+            block = 2 * GROUPS * CHUNK
+            far[...] = jnp.dot(
+                place[pl.ds(pl.multiple_of(j * block, block), block), :],
+                two_in[it].reshape(slots, 128),
+                preferred_element_type=F32,
+            )
+            for number in range(4):
+                way, h = number // 2, number % 2
+                r = pl.multiple_of(way * HALF + j * CHUNK, CHUNK)
+                rows, lanes = unit(r, h)
+                first = (way * GROUPS + 8 * h) * CHUNK
+                strips = [far[first + CHUNK * g : first + CHUNK * (g + 1), :] for g in range(8)]
+                for s, flow in enumerate(swap_blocks(strips)):
+                    value = near[s, rows, lanes] + FAR_SCALE * flow
+                    labor[s, rows, lanes] = value
+                    ext[2 * it + 1, s, pl.ds(HALF + r, CHUNK), lanes] = value.astype(BF16)
+            send_rows(2 * it + 1, j)
             return carry
 
-        over_cells(labor_cells, 2 * it + 1, 0, 4)
+        lax.fori_loop(0, STEPS, labor_step, 0)
         if it == 0:
             make_bands(1)
         if it == ITERS - 1:
-            total_all().wait_recv()
-            sums = jnp.sum(jnp.sum(total_in[...], axis=0), axis=1, keepdims=True)
+            last_copy().wait_recv()
+            sums = jnp.sum(last_in[0] + last_in[1], axis=1, keepdims=True)
             people_all = sums[0:1, 0:1]
             transfers = [sums[1 + k : 2 + k, 0:1] / people_all for k in range(ITERS)]
 
@@ -573,7 +625,7 @@
             for s in range(SECTORS):
                 power = -BETA_WAGE * jnp.log(1.0 + labor[s, rows, lanes])
                 for t in range(SECTORS):
-                    power = power + scalar_ref[24 + SECTORS * s + t] * logs[t]
+                    power = power + mixing_ref[s, t] * logs[t]
                 if it == ITERS - 1:
                     power_ref[s, rows, lanes] = power
                 else:
@@ -598,9 +650,10 @@
 
     for a in range(ITERS + 1):
         first_all(a).wait_send()
-        second_all(a).wait_send()
+        second_copy(a).wait_send()
     sum_all().wait_send()
     total_all().wait_send()
+    last_copy().wait_send()
 
 
 def body(
@@ -620,32 +673,20 @@
     tiles_y = lax.axis_size("gy")
     tiles_x = lax.axis_size("gx")
     slots = tiles_y * tiles_x * CAP
+    chips = tiles_y * tiles_x // 2
     far_pairs = pair_src.shape[0]
-    dest = pair_dest[:, 0]
-    pairs = jnp.stack(
-        [
-            dest,
-            (dest % tiles_x) * (tiles_y * CAP) + (dest // tiles_x) * CAP,
-            (pair_src % GROUPS) * ROWS + pair_src // GROUPS,
-            pair_dst // GROUPS,
-            pair_dst % GROUPS,
-            pair_count,
-        ],
-        axis=0,
-    ).astype(F32)
-    pairs = jnp.pad(pairs, ((0, 122), (0, 0)))
     vmem = pl.BlockSpec(memory_space=pltpu.VMEM)
-    smem = pl.BlockSpec(memory_space=pltpu.SMEM)
+    whole = pl.BlockSpec(memory_space=pl.ANY)
+    smem = pltpu.SMEM
     exchanges = 2 * ITERS
     dma = pltpu.SemaphoreType.DMA
-    scalars = jnp.concatenate([tax_rate, commute_decay, spill_decay, mixing.reshape(-1)])
     power, square = pl.pallas_call(
         functools.partial(kernel, tiles_y, tiles_x),
         out_shape=(
             jax.ShapeDtypeStruct(base_prod.shape, F32),
             jax.ShapeDtypeStruct(resident.shape, F32),
         ),
-        in_specs=[vmem] * 5 + [smem],
+        in_specs=[vmem] * 8 + [whole] * 4,
         out_specs=(vmem, vmem),
         scratch_shapes=[
             pltpu.VMEM((exchanges, SECTORS, ROWS + 2 * HALF, COLS), BF16),
@@ -662,17 +703,23 @@
             pltpu.VMEM((far_pairs, GROUPS * ROWS), BF16),
             pltpu.VMEM((slots, far_pairs), BF16),
             pltpu.VMEM((GROUPS * ROWS, slots), BF16),
-            pltpu.VMEM((GROUPS * ROWS, 128), F32),
-            pltpu.VMEM((ITERS + 1, tiles_x, tiles_y * CAP, 128), BF16),
-            pltpu.VMEM((ITERS + 1, tiles_x, tiles_y * CAP, 128), BF16),
-            pltpu.VMEM((ITERS + 1, tiles_y, tiles_x * CAP, 128), BF16),
-            pltpu.VMEM((ITERS + 1, tiles_y, tiles_x * CAP, 128), BF16),
+            pltpu.VMEM((2 * GROUPS * CHUNK, 128), F32),
+            pltpu.VMEM((ITERS + 1, chips, 2 * CAP, 128), BF16),
+            pltpu.VMEM((ITERS + 1, chips, 2 * CAP, 128), BF16),
+            pltpu.VMEM((ITERS + 1, chips * CAP, 128), BF16),
+            pltpu.VMEM((ITERS + 1, 2, chips * CAP, 128), BF16),
             pltpu.VMEM((8, 128), F32),
-            pltpu.VMEM((tiles_x, 8, 128), F32),
+            pltpu.VMEM((tiles_x // 2, 8, 128), F32),
             pltpu.VMEM((8, 128), F32),
             pltpu.VMEM((tiles_y, 8, 128), F32),
             pltpu.VMEM((ROWS, COLS), F32),
             pltpu.VMEM((ITERS, ROWS, COLS), F32),
+            pltpu.VMEM((2, 8, 128), F32),
+            smem((8,), F32),
+            smem((SECTORS,), F32),
+            smem((SECTORS,), F32),
+            smem((SECTORS, SECTORS), F32),
+            dma((4,)),
             dma((exchanges, 2)),
             dma((exchanges, 2, STEPS)),
             dma((exchanges, 2)),
@@ -681,8 +728,8 @@
             dma((ITERS + 1,)),
             dma((ITERS + 1,)),
             dma((ITERS + 1,)),
-            dma((2,)),
-            dma((2,)),
+            dma((3,)),
+            dma((3,)),
         ],
         compiler_params=pltpu.CompilerParams(
             collective_id=0, has_side_effects=True, vmem_limit_bytes=60 * 1024 * 1024
@@ -692,8 +739,14 @@
         resident,
         floor_space,
         bracket,
-        pairs,
-        scalars,
+        pair_dest.reshape(1, far_pairs),
+        pair_src.reshape(1, far_pairs),
+        pair_dst.reshape(1, far_pairs),
+        pair_count.reshape(1, far_pairs),
+        tax_rate,
+        commute_decay,
+        spill_decay,
+        mixing,
     )
     return base_prod.astype(F32) * jnp.exp(power), jnp.sqrt(square)
 

time: 121 us -> 109 us (0.901)
  Pallas kernels: 113 us -> 106 us
  local copies, waits for them, and re-layouts: 4.34 us -> 0.7 us
    pallas_call x1, Pallas kernels: 113 us -> 106 us  [body(): pl.pallas_call(functools.partial(kernel, tiles_y, tiles_x), out_shape=(ja...]
    unnamed x18 -> x4, local copies, waits for them, and re-layouts: 2.11 us -> 0.01 us
where the time goes in v3:
time: 109 us
  Pallas kernels  106 us (97%)
  other arithmetic  2.38 us (2%)
    pallas_call x1, Pallas kernels, body(): pl.pallas_call(functools.partial(kernel, tiles_y, tiles_x), out_shape=(ja...  106 us
    mul x1, other arithmetic, body(): return (base_prod.astype(F32) * jnp.exp(power), jnp.sqrt(square))  2.38 us

profile of v3, /device:TPU:24, one launch (start us, length us, event | category | flops | bytes accessed | tf_op | source)
XLA Modules:
  0.0 109.3 jit_solution(17591840525311343055)
XLA Ops:
  0.6 0.0 copy-start
  0.6 105.6 %shard_map.131 = (f32[8,128,256]{2,1,0:T(8,128)}, f32[128,256]{1,0:T(8,128)}) custom-call(bf16[8,128,256]{2,1,0:T(8,128)(2,1)} %base_ref.1, f32[128,256]{1,0:T(8,128)} %resident_ref.1, f32[128,256]{1,0:T(8,128)} %floor_ref.1, s32[128,256]{1,0:T(8,128)} %bracket_ref.1, s32[1,512]{1,0:T(1,128)} %bitcast.4, s32[1,512]{1,0:T(1,128)} %bitcast.5, ...), custom_call_target="tpu_custom_call" | custom-call | tf_op jit(solution)/shard_map/pallas_call | solution.py:683
  106.2 0.0 copy-done
  106.2 0.0 copy-start.1
  106.2 2.4 %exponential_multiply_fusion = f32[8,128,256]{2,1,0:T(8,128)} fusion(f32[8,128,256]{2,1,0:T(8,128)} %get-tuple-element.4, bf16[8,128,256]{2,1,0:T(8,128)(2,1)S(1)} %copy-done), kind=kLoop, calls=%fused_computation | loop fusion | flops 524288 | bytes 2621440 | tf_op jit(solution)/shard_map/mul | solution.py:751
  108.6 0.0 copy-done.1
  108.6 0.7 sqrt.3
Async XLA Ops:
  0.6 105.6 %copy-start = (bf16[8,128,256]{2,1,0:T(8,128)(2,1)S(1)}, bf16[8,128,256]{2,1,0:T(8,128)(2,1)}, u32[]{:S(2)}) copy-start(bf16[8,128,256]{2,1,0:T(8,128)(2,1)} %base_ref.1) | copy-start | bytes 1572868
  106.2 2.4 %copy-start.1 = (f32[128,256]{1,0:T(8,128)S(1)}, f32[128,256]{1,0:T(8,128)}, u32[]{:S(2)}) copy-start(f32[128,256]{1,0:T(8,128)} %get-tuple-element.5) | copy-start | bytes 393220

commit v4 on v3

--- a/solution.py
+++ b/solution.py
@@ -37,14 +37,14 @@
 def kernel(
     tiles_y,
     tiles_x,
-    base_ref,
-    resident_ref,
-    floor_ref,
-    bracket_ref,
-    dest_ref,
-    src_ref,
-    dst_ref,
-    count_ref,
+    base_any,
+    resident_any,
+    floor_any,
+    bracket_any,
+    dest_any,
+    src_any,
+    dst_any,
+    count_any,
     tax_any,
     commute_any,
     spill_any,
@@ -77,6 +77,14 @@
     rate_ref,
     income_ref,
     last_in,
+    base_ref,
+    resident_ref,
+    floor_ref,
+    bracket_ref,
+    dest_ref,
+    src_ref,
+    dst_ref,
+    count_ref,
     tax_ref,
     commute_ref,
     spill_ref,
@@ -109,6 +117,14 @@
         pltpu.make_async_copy(source, target, load_sem.at[k])
         for k, (source, target) in enumerate(
             (
+                (base_any, base_ref),
+                (resident_any, resident_ref),
+                (bracket_any, bracket_ref),
+                (floor_any, floor_ref),
+                (dest_any, dest_ref),
+                (src_any, src_ref),
+                (dst_any, dst_ref),
+                (count_any, count_ref),
                 (tax_any, tax_ref),
                 (commute_any, commute_ref),
                 (spill_any, spill_ref),
@@ -676,7 +692,7 @@
     chips = tiles_y * tiles_x // 2
     far_pairs = pair_src.shape[0]
     vmem = pl.BlockSpec(memory_space=pltpu.VMEM)
-    whole = pl.BlockSpec(memory_space=pl.ANY)
+    whole = pl.BlockSpec(memory_space=pltpu.HBM)
     smem = pltpu.SMEM
     exchanges = 2 * ITERS
     dma = pltpu.SemaphoreType.DMA
@@ -686,7 +702,7 @@
             jax.ShapeDtypeStruct(base_prod.shape, F32),
             jax.ShapeDtypeStruct(resident.shape, F32),
         ),
-        in_specs=[vmem] * 8 + [whole] * 4,
+        in_specs=[whole] * 12,
         out_specs=(vmem, vmem),
         scratch_shapes=[
             pltpu.VMEM((exchanges, SECTORS, ROWS + 2 * HALF, COLS), BF16),
@@ -715,11 +731,19 @@
             pltpu.VMEM((ROWS, COLS), F32),
             pltpu.VMEM((ITERS, ROWS, COLS), F32),
             pltpu.VMEM((2, 8, 128), F32),
+            pltpu.VMEM((SECTORS, ROWS, COLS), BF16),
+            pltpu.VMEM((ROWS, COLS), F32),
+            pltpu.VMEM((ROWS, COLS), F32),
+            pltpu.VMEM((ROWS, COLS), jnp.int32),
+            pltpu.VMEM((1, far_pairs), jnp.int32),
+            pltpu.VMEM((1, far_pairs), jnp.int32),
+            pltpu.VMEM((1, far_pairs), jnp.int32),
+            pltpu.VMEM((1, far_pairs), jnp.int32),
             smem((8,), F32),
             smem((SECTORS,), F32),
             smem((SECTORS,), F32),
             smem((SECTORS, SECTORS), F32),
-            dma((4,)),
+            dma((12,)),
             dma((exchanges, 2)),
             dma((exchanges, 2, STEPS)),
             dma((exchanges, 2)),
@@ -732,21 +756,26 @@
             dma((3,)),
         ],
         compiler_params=pltpu.CompilerParams(
-            collective_id=0, has_side_effects=True, vmem_limit_bytes=60 * 1024 * 1024
+            collective_id=0, has_side_effects=True, vmem_limit_bytes=40 * 1024 * 1024
         ),
     )(
-        base_prod,
-        resident,
-        floor_space,
-        bracket,
-        pair_dest.reshape(1, far_pairs),
-        pair_src.reshape(1, far_pairs),
-        pair_dst.reshape(1, far_pairs),
-        pair_count.reshape(1, far_pairs),
-        tax_rate,
-        commute_decay,
-        spill_decay,
-        mixing,
+        *(
+            pltpu.with_memory_space_constraint(x, pltpu.HBM)
+            for x in (
+                base_prod,
+                resident,
+                floor_space,
+                bracket,
+                pair_dest.reshape(1, far_pairs),
+                pair_src.reshape(1, far_pairs),
+                pair_dst.reshape(1, far_pairs),
+                pair_count.reshape(1, far_pairs),
+                tax_rate,
+                commute_decay,
+                spill_decay,
+                mixing,
+            )
+        )
     )
     return base_prod.astype(F32) * jnp.exp(power), jnp.sqrt(square)
 

time: 109 us -> 106 us (0.972)
  Pallas kernels: 106 us -> 103 us
  other arithmetic: 2.38 us -> 1.12 us
    pallas_call x1, Pallas kernels: 106 us -> 103 us  [body(): pl.pallas_call(functools.partial(kernel, tiles_y, tiles_x), out_shape=(ja...]
    mul x1, other arithmetic: 2.38 us -> 1.12 us  [body(): return (base_prod.astype(F32) * jnp.exp(power), jnp.sqrt(square))]
where the time goes in v4:
time: 106 us
  Pallas kernels  103 us (97%)
  other arithmetic  1.12 us (1%)
    pallas_call x1, Pallas kernels, body(): pl.pallas_call(functools.partial(kernel, tiles_y, tiles_x), out_shape=(ja...  103 us

profile of v4, /device:TPU:24, one launch (start us, length us, event | category | flops | bytes accessed | tf_op | source)
XLA Modules:
  0.0 106.0 jit_solution(18222179115453875596)
XLA Ops:
  0.6 0.0 copy-start
  0.6 103.5 %shard_map.131 = (f32[8,128,256]{2,1,0:T(8,128)S(1)}, f32[128,256]{1,0:T(8,128)S(1)}) custom-call(bf16[8,128,256]{2,1,0:T(8,128)(2,1)} %base_any.1, f32[128,256]{1,0:T(8,128)} %resident_any.1, f32[128,256]{1,0:T(8,128)} %floor_any.1, s32[128,256]{1,0:T(8,128)} %bracket_any.1, s32[1,512]{1,0:T(1,128)} %bitcast.4, s32[1,512]{1,0:T(1,128)} %bitcast.5, ...), custom_call_target="tpu_custom_call" | custom-call | tf_op jit(solution)/shard_map/pallas_call | solution.py:699
  104.1 0.0 copy-done
  104.2 1.1 %exponential_multiply_fusion = f32[8,128,256]{2,1,0:T(8,128)} fusion(f32[8,128,256]{2,1,0:T(8,128)S(1)} %get-tuple-element.4, bf16[8,128,256]{2,1,0:T(8,128)(2,1)S(1)} %copy-done), kind=kLoop, calls=%fused_computation | loop fusion | flops 524288 | bytes 2621440 | tf_op jit(solution)/shard_map/mul | solution.py:780
  105.3 0.7 sqrt.3
Async XLA Ops:
  0.6 103.5 %copy-start = (bf16[8,128,256]{2,1,0:T(8,128)(2,1)S(1)}, bf16[8,128,256]{2,1,0:T(8,128)(2,1)}, u32[]{:S(2)}) copy-start(bf16[8,128,256]{2,1,0:T(8,128)(2,1)} %base_any.1) | copy-start | bytes 1572868

commit v5 on v4

--- a/solution.py
+++ b/solution.py
@@ -251,7 +251,18 @@
 
         lax.fori_loop(0, 2, one, 0)
 
-    def columns_pass(e, kind, result):
+    def columns_start(kind, result):
+        def one(half, carry):
+            for k in range(4):
+                s = 4 * half + k
+                result[s] = jnp.dot(
+                    mid[s], band_col[kind * SECTORS + s], preferred_element_type=F32
+                )
+            return carry
+
+        lax.fori_loop(0, 2, one, 0)
+
+    def columns_finish(e, kind, result):
         def one(half, carry):
             for way in range(2):
 
@@ -261,16 +272,13 @@
 
             for k in range(4):
                 s = 4 * half + k
-                i = 2 * half + k // 2
-                b = kind * SECTORS + s
-                value = jnp.dot(mid[s], band_col[b], preferred_element_type=F32)
-                value += jnp.dot(
-                    edge_in[e, 0, i], band_edge[b, 0:128, :], preferred_element_type=F32
-                )
-                value += jnp.dot(
-                    edge_in[e, 1, i], band_edge[b, 128:256, :], preferred_element_type=F32
-                )
-                result[s] = value
+                for side in range(2):
+                    lanes = slice(128 * side, 128 * side + 128)
+                    result[s, :, lanes] += jnp.dot(
+                        edge_in[e, side, 2 * half + k // 2],
+                        band_edge[kind * SECTORS + s, side],
+                        preferred_element_type=F32,
+                    )
             return carry
 
         lax.fori_loop(0, 2, one, 0)
@@ -290,19 +298,22 @@
             )
             band_col[b] = jnp.where(inside, circle, 0.0).astype(BF16)
             rest = jnp.where(inside, 0.0, circle)
-            even = jnp.concatenate([rest[128:256], rest[0:128]], axis=0)
-            odd = jnp.concatenate(
-                [rest[192:256], rest[128:192], rest[64:128], rest[0:64]], axis=0
-            )
-            band_edge[b] = jnp.where(lax.rem(s, 2) == 0, even, odd).astype(BF16)
+            swap = lax.rem(s, 2) == 1
+            for side in range(2):
+                block = rest[128 - 128 * side : 256 - 128 * side, 128 * side : 128 * side + 128]
+                turned = jnp.concatenate([block[HALF:], block[:HALF]], axis=0)
+                band_edge[b, side] = jnp.where(swap, turned, block).astype(BF16)
             return carry
 
         lax.fori_loop(0, SECTORS, one, 0)
 
+    def parts_of(a):
+        return 2 if a == 0 else 1
+
     def first_copy(a, y, x):
         return pltpu.make_async_remote_copy(
-            src_ref=one_out.at[a, y * chips_x + x],
-            dst_ref=one_in.at[a, mine],
+            src_ref=one_out.at[a, y * chips_x + x, pl.ds(0, parts_of(a))],
+            dst_ref=one_in.at[a, mine, pl.ds(0, parts_of(a))],
             send_sem=one_send.at[a],
             recv_sem=one_recv.at[a],
             device_id=(y, 2 * x + core),
@@ -311,8 +322,8 @@
 
     def first_all(a):
         return pltpu.make_async_remote_copy(
-            src_ref=one_out.at[a, pl.ds(0, chips - 1)],
-            dst_ref=one_in.at[a, pl.ds(0, chips - 1)],
+            src_ref=one_out.at[a, pl.ds(0, chips - 1), pl.ds(0, parts_of(a))],
+            dst_ref=one_in.at[a, pl.ds(0, chips - 1), pl.ds(0, parts_of(a))],
             send_sem=one_send.at[a],
             recv_sem=one_recv.at[a],
             device_id=(my, sibling),
@@ -321,8 +332,8 @@
 
     def second_copy(a):
         return pltpu.make_async_remote_copy(
-            src_ref=two_out.at[a],
-            dst_ref=two_in.at[a, 1],
+            src_ref=two_out.at[a, pl.ds(0, parts_of(a))],
+            dst_ref=two_in.at[a, pl.ds(0, parts_of(a)), 1],
             send_sem=two_send.at[a],
             recv_sem=two_recv.at[a],
             device_id=(my, sibling),
@@ -330,20 +341,31 @@
         )
 
     def start_first(a):
+        for k in range(1, chips_x):
+            first_copy(a, my, lax.rem(chip_x + k, chips_x)).start()
+
         def one(j, carry):
-            first_copy(a, *chip_at(j)).start()
+            for k in range(chips_x):
+                first_copy(a, lax.rem(my + j, tiles_y), lax.rem(chip_x + k, chips_x)).start()
             return carry
 
-        lax.fori_loop(1, chips, one, 0)
-        one_in[a, mine] = one_out[a, mine]
+        lax.fori_loop(1, tiles_y, one, 0)
+        for part in range(parts_of(a)):
+            one_in[a, mine, part] = one_out[a, mine, part]
 
     def pass_on(a):
         first_all(a).wait_recv()
-        parts = one_in[a].astype(F32).reshape(chips, 2, CAP, 128)
-        low, high = parts[:, 0], parts[:, 1]
-        two_out[a] = jnp.where(core == 0, high, low).reshape(chips * CAP, 128).astype(BF16)
+        kept = []
+        for part in range(parts_of(a)):
+            parts = one_in[a, :, part].astype(F32).reshape(chips, 2, CAP, 128)
+            low, high = parts[:, 0], parts[:, 1]
+            other = jnp.where(core == 0, high, low).reshape(chips * CAP, 128)
+            two_out[a, part] = other.astype(BF16)
+            own = jnp.where(core == 0, low, high).reshape(chips * CAP, 128)
+            kept.append(own.astype(BF16))
         second_copy(a).start()
-        two_in[a, 0] = jnp.where(core == 0, low, high).reshape(chips * CAP, 128).astype(BF16)
+        for part in range(parts_of(a)):
+            two_in[a, part, 0] = kept[part]
 
     def sum_copy(x):
         return pltpu.make_async_remote_copy(
@@ -436,7 +458,7 @@
     def gather(a):
         picked = jnp.dot(source_hot[...], table[...], preferred_element_type=F32).astype(BF16)
         ordered = jnp.dot(slot_hot[...], picked, preferred_element_type=F32).astype(BF16)
-        one_out[a] = ordered.reshape(chips, 2 * CAP, 128)
+        one_out[a, :, 0] = ordered.reshape(chips, 2 * CAP, 128)
 
     zero = jnp.zeros((8, 128), F32)
 
@@ -488,12 +510,11 @@
     source_hot[...] = jnp.where(
         strip_ids == across[:, 1:2].astype(jnp.int32), 1.0, 0.0
     ).astype(BF16)
-    one_out[ITERS] = (
+    one_out[0, :, 1] = (
         jnp.dot(slot_hot[...], across.astype(BF16), preferred_element_type=F32)
         .astype(BF16)
         .reshape(chips, 2 * CAP, 128)
     )
-    start_first(ITERS)
     gather(0)
     start_first(0)
 
@@ -524,11 +545,9 @@
     tap_row[...] = (unscaled / jnp.sum(unscaled, axis=1, keepdims=True)).astype(BF16).astype(F32)
     make_bands(0)
 
-    pass_on(ITERS)
 
     def build_place():
-        second_copy(ITERS).wait_recv()
-        routing = two_in[ITERS].reshape(slots, 128)
+        routing = two_in[0, 1].reshape(slots, 128)
         line = lax.broadcasted_iota(jnp.int32, (16, 128), 0)
         lane = lax.broadcasted_iota(jnp.int32, (16, 128), 1)
         pick = jnp.where((line == 0) & (lane == 2), float(CHUNK), 0.0)
@@ -567,6 +586,7 @@
             lax.fori_loop(1, chips_x, start_sum, 0)
             sum_in[chip_x] = parts
         rows_pass(2 * it, 0)
+        columns_start(0, near)
         pass_on(it)
         if it == ITERS - 1:
             sum_all().wait_recv()
@@ -579,20 +599,20 @@
 
             lax.fori_loop(1, tiles_y, start_total, 0)
             total_in[my] = halfway
-        columns_pass(2 * it, 0, near)
+        columns_finish(2 * it, 0, near)
         if it == ITERS - 1:
             total_all().wait_recv()
             last_in[0] = jnp.sum(total_in[...], axis=0)
             last_copy().start()
+        second_copy(it).wait_recv()
         if it == 0:
             build_place()
-        second_copy(it).wait_recv()
 
         def labor_step(j, carry):
             block = 2 * GROUPS * CHUNK
             far[...] = jnp.dot(
                 place[pl.ds(pl.multiple_of(j * block, block), block), :],
-                two_in[it].reshape(slots, 128),
+                two_in[it, 0].reshape(slots, 128),
                 preferred_element_type=F32,
             )
             for number in range(4):
@@ -632,7 +652,8 @@
 
             lax.fori_loop(0, ROWS // CHUNK, rent_chunk, 0)
         rows_pass(2 * it + 1, 1)
-        columns_pass(2 * it + 1, 1, near)
+        columns_start(1, near)
+        columns_finish(2 * it + 1, 1, near)
 
         def wage_cells(r, h, revenue):
             rows, lanes = unit(r, h)
@@ -664,7 +685,7 @@
             def _():
                 edge_drain(e, way).wait_send()
 
-    for a in range(ITERS + 1):
+    for a in range(ITERS):
         first_all(a).wait_send()
         second_copy(a).wait_send()
     sum_all().wait_send()
@@ -714,16 +735,16 @@
             pltpu.VMEM((2 * SECTORS, COLS), F32),
             pltpu.VMEM((2 * SECTORS, ROWS, COLS), BF16),
             pltpu.VMEM((2 * SECTORS, COLS, COLS), BF16),
-            pltpu.VMEM((2 * SECTORS, COLS, COLS), BF16),
+            pltpu.VMEM((2 * SECTORS, 2, 128, 128), BF16),
             pltpu.VMEM((GROUPS * ROWS, 128), BF16),
             pltpu.VMEM((far_pairs, GROUPS * ROWS), BF16),
             pltpu.VMEM((slots, far_pairs), BF16),
             pltpu.VMEM((GROUPS * ROWS, slots), BF16),
             pltpu.VMEM((2 * GROUPS * CHUNK, 128), F32),
-            pltpu.VMEM((ITERS + 1, chips, 2 * CAP, 128), BF16),
-            pltpu.VMEM((ITERS + 1, chips, 2 * CAP, 128), BF16),
-            pltpu.VMEM((ITERS + 1, chips * CAP, 128), BF16),
-            pltpu.VMEM((ITERS + 1, 2, chips * CAP, 128), BF16),
+            pltpu.VMEM((ITERS, chips, 2, 2 * CAP, 128), BF16),
+            pltpu.VMEM((ITERS, chips, 2, 2 * CAP, 128), BF16),
+            pltpu.VMEM((ITERS, 2, chips * CAP, 128), BF16),
+            pltpu.VMEM((ITERS, 2, 2, chips * CAP, 128), BF16),
             pltpu.VMEM((8, 128), F32),
             pltpu.VMEM((tiles_x // 2, 8, 128), F32),
             pltpu.VMEM((8, 128), F32),
@@ -748,10 +769,10 @@
             dma((exchanges, 2, STEPS)),
             dma((exchanges, 2)),
             dma((exchanges, 2, 2)),
-            dma((ITERS + 1,)),
-            dma((ITERS + 1,)),
-            dma((ITERS + 1,)),
-            dma((ITERS + 1,)),
+            dma((ITERS,)),
+            dma((ITERS,)),
+            dma((ITERS,)),
+            dma((ITERS,)),
             dma((3,)),
             dma((3,)),
         ],

time: 106 us -> 103 us (0.972)
  Pallas kernels: 103 us -> 101 us
    pallas_call x1, Pallas kernels: 103 us -> 101 us  [body(): pl.pallas_call(functools.partial(kernel, tiles_y, tiles_x), out_shape=(ja...]
where the time goes in v5:
time: 103 us
  Pallas kernels  101 us (98%)
  other arithmetic  1.12 us (1%)
    pallas_call x1, Pallas kernels, body(): pl.pallas_call(functools.partial(kernel, tiles_y, tiles_x), out_shape=(ja...  101 us

profile of v5, /device:TPU:24, one launch (start us, length us, event | category | flops | bytes accessed | tf_op | source)
XLA Modules:
  0.0 103.1 jit_solution(15802424466496523087)
XLA Ops:
  0.6 0.0 copy-start
  0.6 100.7 %shard_map.131 = (f32[8,128,256]{2,1,0:T(8,128)S(1)}, f32[128,256]{1,0:T(8,128)S(1)}) custom-call(bf16[8,128,256]{2,1,0:T(8,128)(2,1)} %base_any.1, f32[128,256]{1,0:T(8,128)} %resident_any.1, f32[128,256]{1,0:T(8,128)} %floor_any.1, s32[128,256]{1,0:T(8,128)} %bracket_any.1, s32[1,512]{1,0:T(1,128)} %bitcast.4, s32[1,512]{1,0:T(1,128)} %bitcast.5, ...), custom_call_target="tpu_custom_call" | custom-call | tf_op jit(solution)/shard_map/pallas_call | solution.py:720
  101.3 0.0 copy-done
  101.3 1.1 %exponential_multiply_fusion = f32[8,128,256]{2,1,0:T(8,128)} fusion(f32[8,128,256]{2,1,0:T(8,128)S(1)} %get-tuple-element.4, bf16[8,128,256]{2,1,0:T(8,128)(2,1)S(1)} %copy-done), kind=kLoop, calls=%fused_computation | loop fusion | flops 524288 | bytes 2621440 | tf_op jit(solution)/shard_map/mul | solution.py:801
  102.4 0.7 sqrt.3
Async XLA Ops:
  0.6 100.7 %copy-start = (bf16[8,128,256]{2,1,0:T(8,128)(2,1)S(1)}, bf16[8,128,256]{2,1,0:T(8,128)(2,1)}, u32[]{:S(2)}) copy-start(bf16[8,128,256]{2,1,0:T(8,128)(2,1)} %base_any.1) | copy-start | bytes 1572868

commit v6 on v5

--- a/solution.py
+++ b/solution.py
@@ -19,6 +19,7 @@
 PAIRS2 = SECTORS // 2
 CHUNK = 16
 STEPS = HALF // CHUNK
+PARTS = ((0, 3), (3, 1))
 MESH = pl.DeviceIdType.MESH
 F32 = jnp.float32
 BF16 = jnp.bfloat16
@@ -152,19 +153,25 @@
     greet(my, beyond)
     lax.fori_loop(1, chips, greet_chip, 0)
 
-    def row_copy(e, j, way):
+    def row_copy(e, way, sectors, j, height, slot):
         start = HALF if way == 0 else ROWS
         land = HALF + ROWS if way == 0 else 0
         target = my - 1 if way == 0 else my + 1
-        step = pl.multiple_of(j * CHUNK, CHUNK)
-        return pltpu.make_async_remote_copy(
-            src_ref=ext.at[e, :, pl.ds(start + step, CHUNK), :],
-            dst_ref=ext.at[e, :, pl.ds(land + step, CHUNK), :],
+        step = pl.multiple_of(j * height, height)
+        return pltpu.make_async_remote_copy(
+            src_ref=ext.at[e, sectors, pl.ds(start + step, height), :],
+            dst_ref=ext.at[e, sectors, pl.ds(land + step, height), :],
             send_sem=row_send.at[e, way],
-            recv_sem=row_recv.at[e, way, j],
+            recv_sem=row_recv.at[e, way, slot],
             device_id=(target, mx),
             device_id_type=MESH,
         )
+
+    def row_step(e, way, j):
+        return row_copy(e, way, pl.ds(0, 2 * PARTS[0][1]), j, CHUNK, j)
+
+    def row_rest(e, way):
+        return row_copy(e, way, pl.ds(2 * PARTS[1][0], 2 * PARTS[1][1]), 0, HALF, STEPS)
 
     def row_drain(e, way):
         start = HALF if way == 0 else ROWS
@@ -186,23 +193,34 @@
 
             @pl.when(can_row[way])
             def _():
-                row_copy(e, j, way).start()
-
-    def wait_rows(e):
+                row_step(e, way, j).start()
+
+    def send_rest(e):
+        for way in range(2):
+
+            @pl.when(can_row[way])
+            def _():
+                row_rest(e, way).start()
+
+    def wait_rows(e, part):
         for way in range(2):
 
             @pl.when(can_row[1 - way])
             def _():
-                for j in range(STEPS):
-                    row_copy(e, j, way).wait_recv()
-
-    def edge_copy(e, i, way):
+                if part == 0:
+                    for j in range(STEPS):
+                        row_step(e, way, j).wait_recv()
+                else:
+                    row_rest(e, way).wait_recv()
+
+    def edge_copy(e, part, way):
         target = mx - 1 if way == 0 else mx + 1
-        return pltpu.make_async_remote_copy(
-            src_ref=edge_out.at[e, way, pl.ds(2 * i, 2)],
-            dst_ref=edge_in.at[e, 1 - way, pl.ds(2 * i, 2)],
+        pairs = pl.ds(*PARTS[part])
+        return pltpu.make_async_remote_copy(
+            src_ref=edge_out.at[e, way, pairs],
+            dst_ref=edge_in.at[e, 1 - way, pairs],
             send_sem=edge_send.at[e, way],
-            recv_sem=edge_recv.at[e, way, i],
+            recv_sem=edge_recv.at[e, way, part],
             device_id=(my, target),
             device_id_type=MESH,
         )
@@ -221,11 +239,9 @@
     lane128 = lax.broadcasted_iota(jnp.int32, (ROWS, 128), 1)
 
     def rows_pass(e, kind):
-        wait_rows(e)
-
-        def one(half, carry):
-            for k in range(2):
-                i = 2 * half + k
+        for part, (first_pair, count) in enumerate(PARTS):
+            wait_rows(e, part)
+            for i in range(first_pair, first_pair + count):
                 ends = []
                 for s in (2 * i, 2 * i + 1):
                     passed = jnp.dot(
@@ -245,11 +261,7 @@
 
                 @pl.when(can_edge[way])
                 def _():
-                    edge_copy(e, half, way).start()
-
-            return carry
-
-        lax.fori_loop(0, 2, one, 0)
+                    edge_copy(e, part, way).start()
 
     def columns_start(kind, result):
         def one(half, carry):
@@ -263,25 +275,21 @@
         lax.fori_loop(0, 2, one, 0)
 
     def columns_finish(e, kind, result):
-        def one(half, carry):
+        for part, (first_pair, count) in enumerate(PARTS):
             for way in range(2):
 
                 @pl.when(can_edge[1 - way])
                 def _():
-                    edge_copy(e, half, way).wait_recv()
-
-            for k in range(4):
-                s = 4 * half + k
+                    edge_copy(e, part, way).wait_recv()
+
+            for s in range(2 * first_pair, 2 * (first_pair + count)):
                 for side in range(2):
                     lanes = slice(128 * side, 128 * side + 128)
                     result[s, :, lanes] += jnp.dot(
-                        edge_in[e, side, 2 * half + k // 2],
+                        edge_in[e, side, s // 2],
                         band_edge[kind * SECTORS + s, side],
                         preferred_element_type=F32,
                     )
-            return carry
-
-        lax.fori_loop(0, 2, one, 0)
 
     def make_bands(kind):
         u = lax.broadcasted_iota(jnp.int32, (COLS, COLS), 0)
@@ -437,7 +445,10 @@
                 send_rows(sent, j)
             return carry
 
-        return lax.fori_loop(0, STEPS, step, carry)
+        carry = lax.fori_loop(0, STEPS, step, carry)
+        if sent is not None:
+            send_rest(sent)
+        return carry
 
     def shares(it, r, h, wages, revenue):
         rows, lanes = unit(r, h)
@@ -481,6 +492,7 @@
     pl.semaphore_wait(barrier, chips + 1)
     for j in range(STEPS):
         send_rows(0, j)
+    send_rest(0)
 
     line = lax.broadcasted_iota(jnp.int32, (8, far_pairs), 0)
     source, target = src_ref[...], dst_ref[...]
@@ -629,6 +641,7 @@
             return carry
 
         lax.fori_loop(0, STEPS, labor_step, 0)
+        send_rest(2 * it + 1)
         if it == 0:
             make_bands(1)
         if it == ITERS - 1:
@@ -766,7 +779,7 @@
             smem((SECTORS, SECTORS), F32),
             dma((12,)),
             dma((exchanges, 2)),
-            dma((exchanges, 2, STEPS)),
+            dma((exchanges, 2, STEPS + 1)),
             dma((exchanges, 2)),
             dma((exchanges, 2, 2)),
             dma((ITERS,)),

time: 103 us -> 101 us (0.981)
  Pallas kernels: 101 us -> 98 us
    pallas_call x1, Pallas kernels: 101 us -> 98 us  [body(): pl.pallas_call(functools.partial(kernel, tiles_y, tiles_x), out_shape=(ja...]
where the time goes in v6:
time: 101 us; the launch traced here: 100 us
  Pallas kernels  98 us (97%)
  other arithmetic  1.12 us (1%)
    pallas_call x1, Pallas kernels, body(): pl.pallas_call(functools.partial(kernel, tiles_y, tiles_x), out_shape=(ja...  98 us

profile of v6, /device:TPU:24, one launch (start us, length us, event | category | flops | bytes accessed | tf_op | source)
XLA Modules:
  0.0 100.5 jit_solution(6136574701941154175)
XLA Ops:
  0.6 0.0 copy-start
  0.6 98.0 %shard_map.131 = (f32[8,128,256]{2,1,0:T(8,128)S(1)}, f32[128,256]{1,0:T(8,128)S(1)}) custom-call(bf16[8,128,256]{2,1,0:T(8,128)(2,1)} %base_any.1, f32[128,256]{1,0:T(8,128)} %resident_any.1, f32[128,256]{1,0:T(8,128)} %floor_any.1, s32[128,256]{1,0:T(8,128)} %bracket_any.1, s32[1,512]{1,0:T(1,128)} %bitcast.4, s32[1,512]{1,0:T(1,128)} %bitcast.5, ...), custom_call_target="tpu_custom_call" | custom-call | tf_op jit(solution)/shard_map/pallas_call | solution.py:733
  98.7 0.0 copy-done
  98.7 1.1 %exponential_multiply_fusion = f32[8,128,256]{2,1,0:T(8,128)} fusion(f32[8,128,256]{2,1,0:T(8,128)S(1)} %get-tuple-element.4, bf16[8,128,256]{2,1,0:T(8,128)(2,1)S(1)} %copy-done), kind=kLoop, calls=%fused_computation | loop fusion | flops 524288 | bytes 2621440 | tf_op jit(solution)/shard_map/mul | solution.py:814
  99.8 0.7 sqrt.3
Async XLA Ops:
  0.6 98.0 %copy-start = (bf16[8,128,256]{2,1,0:T(8,128)(2,1)S(1)}, bf16[8,128,256]{2,1,0:T(8,128)(2,1)}, u32[]{:S(2)}) copy-start(bf16[8,128,256]{2,1,0:T(8,128)(2,1)} %base_any.1) | copy-start | bytes 1572868

commit v7 on v6

--- a/solution.py
+++ b/solution.py
@@ -168,10 +168,10 @@
         )
 
     def row_step(e, way, j):
-        return row_copy(e, way, pl.ds(0, 2 * PARTS[0][1]), j, CHUNK, j)
+        return row_copy(e, way, pl.ds(0, 2 * PARTS[0][1]), j, CHUNK, 0)
 
     def row_rest(e, way):
-        return row_copy(e, way, pl.ds(2 * PARTS[1][0], 2 * PARTS[1][1]), 0, HALF, STEPS)
+        return row_copy(e, way, pl.ds(2 * PARTS[1][0], 2 * PARTS[1][1]), 0, HALF, 1)
 
     def row_drain(e, way):
         start = HALF if way == 0 else ROWS
@@ -208,8 +208,7 @@
             @pl.when(can_row[1 - way])
             def _():
                 if part == 0:
-                    for j in range(STEPS):
-                        row_step(e, way, j).wait_recv()
+                    row_copy(e, way, pl.ds(0, 2 * PARTS[0][1]), 0, HALF, 0).wait_recv()
                 else:
                     row_rest(e, way).wait_recv()
 
@@ -455,10 +454,11 @@
         powers = [w * w * w for w in wages]
         inverse = 1.0 / sum(powers[1:], powers[0])
         people = resident_ref[rows, lanes]
-        share = [p * inverse for p in powers]
-        income = sum([q * w for q, w in zip(share[1:], wages[1:])], share[0] * wages[0])
+        earned = sum([p * w for p, w in zip(powers[1:], wages[1:])], powers[0] * wages[0])
+        income = earned * inverse
         income_ref[it, rows, lanes] = income
-        supply = [people * q for q in share]
+        scale = people * inverse
+        supply = [p * scale for p in powers]
         for s in range(SECTORS):
             ext[2 * it, s, pl.ds(HALF + r, CHUNK), lanes] = supply[s].astype(BF16)
         for g, strip in enumerate(swap_blocks(supply)):
@@ -685,7 +685,7 @@
             return revenue
 
         sent = 2 * it + 2 if it < ITERS - 1 else None
-        revenues.append(over_cells(wage_cells, sent, zero, 2))
+        revenues.append(over_cells(wage_cells, sent, zero, 4))
 
     for e in range(2 * ITERS):
         for way in range(2):
@@ -779,7 +779,7 @@
             smem((SECTORS, SECTORS), F32),
             dma((12,)),
             dma((exchanges, 2)),
-            dma((exchanges, 2, STEPS + 1)),
+            dma((exchanges, 2, 2)),
             dma((exchanges, 2)),
             dma((exchanges, 2, 2)),
             dma((ITERS,)),

time: 101 us -> 98.8 us (0.978)
  Pallas kernels: 98 us -> 96.2 us
    pallas_call x1, Pallas kernels: 98 us -> 96.2 us  [body(): pl.pallas_call(functools.partial(kernel, tiles_y, tiles_x), out_shape=(ja...]
where the time goes in v7:
time: 98.8 us; the launch traced here: 98.7 us
  Pallas kernels  96.2 us (97%)
  other arithmetic  1.12 us (1%)
    pallas_call x1, Pallas kernels, body(): pl.pallas_call(functools.partial(kernel, tiles_y, tiles_x), out_shape=(ja...  96.2 us

profile of v7, /device:TPU:24, one launch (start us, length us, event | category | flops | bytes accessed | tf_op | source)
XLA Modules:
  0.0 98.7 jit_solution(17698262925901597323)
XLA Ops:
  0.6 0.0 copy-start
  0.6 96.2 %shard_map.131 = (f32[8,128,256]{2,1,0:T(8,128)S(1)}, f32[128,256]{1,0:T(8,128)S(1)}) custom-call(bf16[8,128,256]{2,1,0:T(8,128)(2,1)} %base_any.1, f32[128,256]{1,0:T(8,128)} %resident_any.1, f32[128,256]{1,0:T(8,128)} %floor_any.1, s32[128,256]{1,0:T(8,128)} %bracket_any.1, s32[1,512]{1,0:T(1,128)} %bitcast.4, s32[1,512]{1,0:T(1,128)} %bitcast.5, ...), custom_call_target="tpu_custom_call" | custom-call | tf_op jit(solution)/shard_map/pallas_call | solution.py:733
  96.9 0.0 copy-done
  96.9 1.1 %exponential_multiply_fusion = f32[8,128,256]{2,1,0:T(8,128)} fusion(f32[8,128,256]{2,1,0:T(8,128)S(1)} %get-tuple-element.4, bf16[8,128,256]{2,1,0:T(8,128)(2,1)S(1)} %copy-done), kind=kLoop, calls=%fused_computation | loop fusion | flops 524288 | bytes 2621440 | tf_op jit(solution)/shard_map/mul | solution.py:814
  98.0 0.7 sqrt.3
Async XLA Ops:
  0.6 96.3 %copy-start = (bf16[8,128,256]{2,1,0:T(8,128)(2,1)S(1)}, bf16[8,128,256]{2,1,0:T(8,128)(2,1)}, u32[]{:S(2)}) copy-start(bf16[8,128,256]{2,1,0:T(8,128)(2,1)} %base_any.1) | copy-start | bytes 1572868

commit v8 on v7

--- a/solution.py
+++ b/solution.py
@@ -138,20 +138,19 @@
 
     barrier = pltpu.get_barrier_semaphore()
 
-    def chip_at(j):
-        return lax.rem(my + j // chips_x, tiles_y), lax.rem(chip_x + lax.rem(j, chips_x), chips_x)
-
     def greet(y, x):
         pl.semaphore_signal(barrier, inc=1, device_id=(y, x), device_id_type=MESH)
 
-    def greet_chip(j, carry):
-        y, x = chip_at(j)
-        greet(y, 2 * x + core)
+    def greet_row(j, carry):
+        for k in range(chips_x):
+            greet(lax.rem(my + j, tiles_y), 2 * lax.rem(chip_x + k, chips_x) + core)
         return carry
 
     greet(my, sibling)
     greet(my, beyond)
-    lax.fori_loop(1, chips, greet_chip, 0)
+    for k in range(1, chips_x):
+        greet(my, 2 * lax.rem(chip_x + k, chips_x) + core)
+    lax.fori_loop(1, tiles_y, greet_row, 0)
 
     def row_copy(e, way, sectors, j, height, slot):
         start = HALF if way == 0 else ROWS
@@ -644,6 +643,14 @@
         send_rest(2 * it + 1)
         if it == 0:
             make_bands(1)
+
+        def labor_power(c, carry):
+            rows = pl.ds(pl.multiple_of(c * CHUNK, CHUNK), CHUNK)
+            for s in range(SECTORS):
+                labor[s, rows, :] = -BETA_WAGE * jnp.log(1.0 + labor[s, rows, :])
+            return carry
+
+        lax.fori_loop(0, ROWS // CHUNK, labor_power, 0)
         if it == ITERS - 1:
             last_copy().wait_recv()
             sums = jnp.sum(last_in[0] + last_in[1], axis=1, keepdims=True)
@@ -673,7 +680,7 @@
             logs = [jnp.log(1.0 + near[s, rows, lanes]) for s in range(SECTORS)]
             wages = []
             for s in range(SECTORS):
-                power = -BETA_WAGE * jnp.log(1.0 + labor[s, rows, lanes])
+                power = labor[s, rows, lanes]
                 for t in range(SECTORS):
                     power = power + mixing_ref[s, t] * logs[t]
                 if it == ITERS - 1:

time: 98.8 us -> 98 us (level)
  no operation moved by 1% of the time
where the time goes in v8:
time: 98 us; the launch traced here: 97.9 us
  Pallas kernels  95.4 us (97%)
  other arithmetic  1.12 us (1%)
    pallas_call x1, Pallas kernels, body(): pl.pallas_call(functools.partial(kernel, tiles_y, tiles_x), out_shape=(ja...  95.4 us

profile of v8, /device:TPU:24, one launch (start us, length us, event | category | flops | bytes accessed | tf_op | source)
XLA Modules:
  0.0 97.9 jit_solution(12945754417509897288)
XLA Ops:
  0.6 0.0 copy-start
  0.6 95.4 %shard_map.131 = (f32[8,128,256]{2,1,0:T(8,128)S(1)}, f32[128,256]{1,0:T(8,128)S(1)}) custom-call(bf16[8,128,256]{2,1,0:T(8,128)(2,1)} %base_any.1, f32[128,256]{1,0:T(8,128)} %resident_any.1, f32[128,256]{1,0:T(8,128)} %floor_any.1, s32[128,256]{1,0:T(8,128)} %bracket_any.1, s32[1,512]{1,0:T(1,128)} %bitcast.4, s32[1,512]{1,0:T(1,128)} %bitcast.5, ...), custom_call_target="tpu_custom_call" | custom-call | tf_op jit(solution)/shard_map/pallas_call | solution.py:740
  96.0 0.0 copy-done
  96.0 1.1 %exponential_multiply_fusion = f32[8,128,256]{2,1,0:T(8,128)} fusion(f32[8,128,256]{2,1,0:T(8,128)S(1)} %get-tuple-element.4, bf16[8,128,256]{2,1,0:T(8,128)(2,1)S(1)} %copy-done), kind=kLoop, calls=%fused_computation | loop fusion | flops 524288 | bytes 2621440 | tf_op jit(solution)/shard_map/mul | solution.py:821
  97.2 0.7 sqrt.3
Async XLA Ops:
  0.6 95.4 %copy-start = (bf16[8,128,256]{2,1,0:T(8,128)(2,1)S(1)}, bf16[8,128,256]{2,1,0:T(8,128)(2,1)}, u32[]{:S(2)}) copy-start(bf16[8,128,256]{2,1,0:T(8,128)(2,1)} %base_any.1) | copy-start | bytes 1572868

commit v9 on v8

--- a/solution.py
+++ b/solution.py
@@ -347,15 +347,14 @@
         )
 
     def start_first(a):
-        for k in range(1, chips_x):
-            first_copy(a, my, lax.rem(chip_x + k, chips_x)).start()
-
-        def one(j, carry):
-            for k in range(chips_x):
-                first_copy(a, lax.rem(my + j, tiles_y), lax.rem(chip_x + k, chips_x)).start()
-            return carry
-
-        lax.fori_loop(1, tiles_y, one, 0)
+        def far_first(count):
+            return sorted(range(count), key=lambda d: -min(d % 4, -d % 4) - (d // 4) / 2)
+
+        for j in far_first(tiles_y):
+            y = lax.rem(my + j, tiles_y)
+            for k in far_first(chips_x):
+                if j or k:
+                    first_copy(a, y, lax.rem(chip_x + k, chips_x)).start()
         for part in range(parts_of(a)):
             one_in[a, mine, part] = one_out[a, mine, part]
 

time: 98 us -> 98.1 us (level)
  no operation moved by 1% of the time
where the time goes in v9:
time: 98.1 us; the launch traced here: 98 us
  Pallas kernels  95.5 us (97%)
  other arithmetic  1.12 us (1%)
    pallas_call x1, Pallas kernels, body(): pl.pallas_call(functools.partial(kernel, tiles_y, tiles_x), out_shape=(ja...  95.5 us

profile of v9, /device:TPU:24, one launch (start us, length us, event | category | flops | bytes accessed | tf_op | source)
XLA Modules:
  0.0 98.0 jit_solution(12528604147687688860)
XLA Ops:
  0.6 0.0 copy-start
  0.6 95.5 %shard_map.131 = (f32[8,128,256]{2,1,0:T(8,128)S(1)}, f32[128,256]{1,0:T(8,128)S(1)}) custom-call(bf16[8,128,256]{2,1,0:T(8,128)(2,1)} %base_any.1, f32[128,256]{1,0:T(8,128)} %resident_any.1, f32[128,256]{1,0:T(8,128)} %floor_any.1, s32[128,256]{1,0:T(8,128)} %bracket_any.1, s32[1,512]{1,0:T(1,128)} %bitcast.4, s32[1,512]{1,0:T(1,128)} %bitcast.5, ...), custom_call_target="tpu_custom_call" | custom-call | tf_op jit(solution)/shard_map/pallas_call | solution.py:739
  96.2 0.0 copy-done
  96.2 1.1 %exponential_multiply_fusion = f32[8,128,256]{2,1,0:T(8,128)} fusion(f32[8,128,256]{2,1,0:T(8,128)S(1)} %get-tuple-element.4, bf16[8,128,256]{2,1,0:T(8,128)(2,1)S(1)} %copy-done), kind=kLoop, calls=%fused_computation | loop fusion | flops 524288 | bytes 2621440 | tf_op jit(solution)/shard_map/mul | solution.py:820
  97.3 0.7 sqrt.3
Async XLA Ops:
  0.6 95.5 %copy-start = (bf16[8,128,256]{2,1,0:T(8,128)(2,1)S(1)}, bf16[8,128,256]{2,1,0:T(8,128)(2,1)}, u32[]{:S(2)}) copy-start(bf16[8,128,256]{2,1,0:T(8,128)(2,1)} %base_any.1) | copy-start | bytes 1572868

commit v10 on v8

--- a/solution.py
+++ b/solution.py
@@ -557,8 +557,10 @@
     make_bands(0)
 
 
-    def build_place():
-        routing = two_in[0, 1].reshape(slots, 128)
+    def build_place(half):
+        width = chips * CAP
+        columns = slice(half * width, (half + 1) * width)
+        routing = two_in[0, 1, half]
         line = lax.broadcasted_iota(jnp.int32, (16, 128), 0)
         lane = lax.broadcasted_iota(jnp.int32, (16, 128), 1)
         pick = jnp.where((line == 0) & (lane == 2), float(CHUNK), 0.0)
@@ -567,11 +569,11 @@
         found = lax.dot_general(
             pick, routing, (((1,), (1,)), ((), ())), preferred_element_type=F32
         )
-        where_to, weight = found[0:1, :].astype(jnp.int32), found[1:2, :]
+        where_to, weight = found[0:1, :].astype(jnp.int32), FAR_SCALE * found[1:2, :]
 
         def one(g, carry):
-            strip = g * ROWS + lax.broadcasted_iota(jnp.int32, (ROWS, slots), 0)
-            place[pl.ds(pl.multiple_of(g * ROWS, ROWS), ROWS), :] = jnp.where(
+            strip = g * ROWS + lax.broadcasted_iota(jnp.int32, (ROWS, width), 0)
+            place[pl.ds(pl.multiple_of(g * ROWS, ROWS), ROWS), columns] = jnp.where(
                 strip == where_to, weight, 0.0
             ).astype(BF16)
             return carry
@@ -599,6 +601,8 @@
         rows_pass(2 * it, 0)
         columns_start(0, near)
         pass_on(it)
+        if it == 0:
+            build_place(0)
         if it == ITERS - 1:
             sum_all().wait_recv()
             halfway = jnp.sum(sum_in[...], axis=0)
@@ -617,7 +621,7 @@
             last_copy().start()
         second_copy(it).wait_recv()
         if it == 0:
-            build_place()
+            build_place(1)
 
         def labor_step(j, carry):
             block = 2 * GROUPS * CHUNK
@@ -633,7 +637,7 @@
                 first = (way * GROUPS + 8 * h) * CHUNK
                 strips = [far[first + CHUNK * g : first + CHUNK * (g + 1), :] for g in range(8)]
                 for s, flow in enumerate(swap_blocks(strips)):
-                    value = near[s, rows, lanes] + FAR_SCALE * flow
+                    value = near[s, rows, lanes] + flow
                     labor[s, rows, lanes] = value
                     ext[2 * it + 1, s, pl.ds(HALF + r, CHUNK), lanes] = value.astype(BF16)
             send_rows(2 * it + 1, j)

time: 98 us -> 98.3 us (level)
  no operation moved by 1% of the time
where the time goes in v10:
time: 98.3 us; the launch traced here: 98.1 us
  Pallas kernels  95.7 us (97%)
  other arithmetic  1.12 us (1%)
    pallas_call x1, Pallas kernels, body(): pl.pallas_call(functools.partial(kernel, tiles_y, tiles_x), out_shape=(ja...  95.7 us

profile of v10, /device:TPU:24, one launch (start us, length us, event | category | flops | bytes accessed | tf_op | source)
XLA Modules:
  0.0 98.1 jit_solution(2828383160779425098)
XLA Ops:
  0.6 0.0 copy-start
  0.6 95.7 %shard_map.131 = (f32[8,128,256]{2,1,0:T(8,128)S(1)}, f32[128,256]{1,0:T(8,128)S(1)}) custom-call(bf16[8,128,256]{2,1,0:T(8,128)(2,1)} %base_any.1, f32[128,256]{1,0:T(8,128)} %resident_any.1, f32[128,256]{1,0:T(8,128)} %floor_any.1, s32[128,256]{1,0:T(8,128)} %bracket_any.1, s32[1,512]{1,0:T(1,128)} %bitcast.4, s32[1,512]{1,0:T(1,128)} %bitcast.5, ...), custom_call_target="tpu_custom_call" | custom-call | tf_op jit(solution)/shard_map/pallas_call | solution.py:744
  96.3 0.0 copy-done
  96.3 1.1 %exponential_multiply_fusion = f32[8,128,256]{2,1,0:T(8,128)} fusion(f32[8,128,256]{2,1,0:T(8,128)S(1)} %get-tuple-element.4, bf16[8,128,256]{2,1,0:T(8,128)(2,1)S(1)} %copy-done), kind=kLoop, calls=%fused_computation | loop fusion | flops 524288 | bytes 2621440 | tf_op jit(solution)/shard_map/mul | solution.py:825
  97.5 0.7 sqrt.3
Async XLA Ops:
  0.6 95.7 %copy-start = (bf16[8,128,256]{2,1,0:T(8,128)(2,1)S(1)}, bf16[8,128,256]{2,1,0:T(8,128)(2,1)}, u32[]{:S(2)}) copy-start(bf16[8,128,256]{2,1,0:T(8,128)(2,1)} %base_any.1) | copy-start | bytes 1572868
